TPU v7x, 512 devices: a whole 4x8x8 slice. The times are simulated.
512 devices in a mesh: train: 16 (over x_hi, y), target: 32 (over z, x_lo, core).
Axes of the slice: x: 4 (x_hi: 2, x_lo: 2; x = x_hi * 2 + x_lo), y: 8, z: 8, core: 2. Of those that a mesh axis runs over, the one named last changes fastest.
Arguments:
- train_embed: bfloat16 [16384, 256], P('train'), may hold values from -8 to 8
- train_label: int32 [16384], P('train'), may hold values from 0 to 7
- target_embed: bfloat16 [32768, 256], P('target'), may hold values from -8 to 8
- target_label: int32 [32768], P('target'), may hold values from 0 to 7
- label_cost: float32 [8, 8], replicated, may hold values from 0.1 to 1.5
Outputs:
- value: float32 [16384], P('train')
- target_potential: float32 [32768], P('target')
- barycentre: float32 [16384, 256], P(('train', 'target'))
All inputs are finite; a program needn't handle non-finite values.
Results may differ from a plain program's by a relative error of at most 0.0033.
Values sent between devices are 32-bit elements; how exact they have to be, the bound alone decides.
No kernel may reach another device: no remote copies, remote signals or barrier semaphores. Data moves between devices by JAX's collectives and lax.ppermute only.
A program may use at most 128 MiB of HBM per device.

v0:
```python
import functools
import math

import jax
import jax.numpy as jnp
from jax import lax
from jax.experimental import pallas as pl
from jax.experimental.pallas import tpu as pltpu
from jax.sharding import PartitionSpec as P

EPS = 0.05
SCALE = 128.0
KAPPA = math.log2(math.e) / EPS / SCALE
LOG2 = math.log2(math.e) / EPS
LANES = 256
SHARE = 32
CHUNK = 2 * SHARE + 8


def pieces(v):
    hi = v.astype(jnp.bfloat16).astype(jnp.float32)
    rest = v - hi
    mid = rest.astype(jnp.bfloat16).astype(jnp.float32)
    lo = (rest - mid).astype(jnp.bfloat16).astype(jnp.float32)
    return hi, mid, lo


def tail(first, second):
    n = first[0].shape[1]
    row = lax.broadcasted_iota(jnp.int32, (8, n), 0)
    out = jnp.zeros((8, n), jnp.float32)
    for k, v in enumerate(first + second):
        out = jnp.where(row == k, v, out)
    return out


def ones_like3(v):
    return (jnp.ones_like(v),) * 3


def train_rows(label, phi):
    m = label.shape[1]
    onehot = (lax.broadcasted_iota(jnp.int32, (8, m), 0) == label).astype(jnp.float32)
    last = tail(ones_like3(phi), pieces(phi * SCALE))
    return jnp.concatenate([onehot, onehot, onehot, last], axis=0)


def target_rows(label, gamma, label_cost):
    n = label.shape[1]
    table = jnp.zeros((8, n), jnp.float32)
    for b in range(8):
        table = jnp.where(label == b, label_cost[:, b : b + 1], table)
    last = tail(pieces(gamma * SCALE), ones_like3(gamma))
    return jnp.concatenate(list(pieces(table * -SCALE)) + [last], axis=0)


def as_columns(rows):
    pad = jnp.zeros((96, rows.shape[1]), jnp.float32)
    return jnp.concatenate([rows, pad], axis=0).T.astype(jnp.bfloat16)


def as_rows(rows):
    pad = jnp.zeros((96, rows.shape[1]), jnp.float32)
    return jnp.concatenate([rows, pad], axis=0).astype(jnp.bfloat16)


def dot_nt(a, b):
    return lax.dot_general(a, b, (((1,), (1,)), ((), ())), preferred_element_type=jnp.float32)


def dot_nn(a, b):
    return lax.dot_general(a, b, (((1,), (0,)), ((), ())), preferred_element_type=jnp.float32)


def square_means(v):
    sums = jnp.sum(jnp.square(v.astype(jnp.float32)), axis=1, keepdims=True)
    return jnp.broadcast_to(sums * (1.0 / v.shape[1]), (v.shape[0], 128))


def to_everyone(v, out_ref):
    for k in range(out_ref.shape[0]):
        out_ref[k] = v


def in_lanes(v):
    return jnp.concatenate([v[k : k + 1] for k in range(v.shape[0])], axis=1)


def tree(parts, combine):
    while len(parts) > 1:
        parts = [combine(parts[k], parts[k + 1]) for k in range(0, len(parts), 2)]
    return parts[0]


def lse_received(ref):
    parts = [ref[k] for k in range(ref.shape[0])]
    top = tree(parts, jnp.maximum)
    total = tree([jnp.exp((part - top) * (1.0 / EPS)) for part in parts], jnp.add)
    return in_lanes(top + EPS * jnp.log(total))


def sum_received(ref):
    return tree([ref[k] for k in range(ref.shape[0])], jnp.add)


def fetch(pairs, sems):
    copies = [pltpu.make_async_copy(src, dst, sems.at[k]) for k, (src, dst) in enumerate(pairs)]
    for copy in copies:
        copy.start()
    return copies


def wait_all(copies):
    for copy in copies:
        copy.wait()


def rows_first(
    x_any, y_any, lx_any, ly_any, lc_any, core_ref,
    out_ref, sqx_ref, sqy_ref, at_ref, x_ref, y_ref, lx_ref, ly_ref, lc_ref, sems,
):
    pairs = [(ly_any, ly_ref), (lc_any, lc_ref), (lx_any, lx_ref), (y_any, y_ref), (x_any, x_ref)]
    copies = fetch(pairs, sems)
    wait_all(copies[:3])
    rows = as_rows(train_rows(lx_ref[...], jnp.zeros(lx_ref.shape, jnp.float32)))
    columns = as_columns(target_rows(ly_ref[...], jnp.zeros(ly_ref.shape, jnp.float32), lc_ref[...]))
    copies[3].wait()
    y = y_ref[...]
    means = square_means(y)
    norms = jnp.concatenate([means * SCALE] * (LANES // 128), axis=1)
    copies[4].wait()
    for k in range(x_ref.shape[0] // LANES):
        at = slice(k * LANES, (k + 1) * LANES)
        t = dot_nt(y, x_ref[at, :]) + dot_nn(columns, rows[:, at]) - norms
        top = jnp.max(t, axis=0, keepdims=True)
        total = jnp.sum(jnp.exp2((t - top) * KAPPA), axis=0, keepdims=True)
        out = top * (1.0 / SCALE) + EPS * jnp.log(total)
        for r in range(LANES // 128):
            row = k * (LANES // 128) + r
            at_ref[row : row + 1, :] = out[:, r * 128 : (r + 1) * 128]
    sqx_ref[...] = square_means(x_ref[...]).T[0:1]
    sqy_ref[...] = means.T[0:1]
    to_everyone(at_ref[...], out_ref)


def in_rows(v):
    return jnp.broadcast_to(v, (128, v.shape[1])).T


def columns_first(log_m, x_ref, y_ref, lx_ref, ly_ref, lc_ref, got_ref, t_ref, out_ref, phi_ref, at_ref):
    zero_m, zero_n = (jnp.zeros(ref.shape, jnp.float32) for ref in (lx_ref, ly_ref))
    phi = -log_m - lse_received(got_ref)
    phi_ref[...] = phi
    down = in_rows(phi * LOG2)
    down = jnp.concatenate([down] * (LANES // 128), axis=1)
    x = x_ref[...]
    columns = as_columns(train_rows(lx_ref[...], zero_m))
    rows = as_rows(target_rows(ly_ref[...], zero_n, lc_ref[...]))
    for k in range(y_ref.shape[0] // LANES):
        at = slice(k * LANES, (k + 1) * LANES)
        t = (dot_nt(x, y_ref[at, :]) + dot_nn(columns, rows[:, at])) * KAPPA
        t_ref[:, at] = t
        t = t + down
        top = jnp.max(t, axis=0, keepdims=True)
        total = jnp.sum(jnp.exp2(t - top), axis=0, keepdims=True)
        out = top * (1.0 / LOG2) + EPS * jnp.log(total)
        for r in range(LANES // 128):
            row = k * (LANES // 128) + r
            at_ref[row : row + 1, :] = out[:, r * 128 : (r + 1) * 128]
    to_everyone(at_ref[...], out_ref)


def rows_next(log_n, t_ref, phi_ref, got_ref, out_ref, gamma_ref, at_ref):
    gamma = -log_n - lse_received(got_ref)
    gamma_ref[...] = gamma
    down = in_rows((phi_ref[...] + log_n) * LOG2)
    across = gamma * LOG2
    for k in range(t_ref.shape[0] // 128):
        rows = slice(k * 128, (k + 1) * 128)
        total = 0.0
        for j in range(t_ref.shape[1] // 128):
            at = slice(j * 128, (j + 1) * 128)
            total = total + jnp.exp2(t_ref[rows, at] + down[rows] + across[:, at])
        at_ref[k : k + 1, :] = jnp.sum(total.T, axis=0, keepdims=True)
    to_everyone(at_ref[...], out_ref)


def columns_next(log_m, log_n, t_ref, phi_ref, gamma_ref, sqx_ref, got_ref, out_ref, new_ref, at_ref):
    n = t_ref.shape[1]
    phi = phi_ref[...] + log_n - log_m - EPS * jnp.log(in_lanes(sum_received(got_ref)))
    new_ref[...] = phi
    down = in_rows(phi * LOG2)
    across = (gamma_ref[...] + log_m) * LOG2
    for k in range(n // 128):
        at = slice(k * 128, (k + 1) * 128)
        at_ref[:, at] = jnp.sum(jnp.exp2(t_ref[:, at] + down + across[:, at]), axis=0, keepdims=True)
    dual_sum = jnp.sum(phi + sqx_ref[...], axis=1, keepdims=True)
    at_ref[:, n : n + 128] = jnp.broadcast_to(dual_sum, (1, 128))
    to_everyone(at_ref[...], out_ref)


def on_diagonal(v):
    shape = (SHARE, 128)
    row, column = (lax.broadcasted_iota(jnp.int32, shape, k) for k in range(2))
    axis = 0 if v.shape[0] == SHARE else 1
    return jnp.sum(jnp.where(row == column, v, 0.0), axis=axis, keepdims=True)


def weighted_sums(shift, relative, t_ref, y_ref, phi_ref, gamma_ref, core_ref, out_ref, down_ref):
    core = core_ref[0]
    n = t_ref.shape[1]
    down_ref[...] = in_rows((phi_ref[...] + shift) * LOG2)
    across = gamma_ref[...] * LOG2
    y = y_ref[...]
    per = min(8, len(relative))
    for b in range(len(relative) // per):
        weights = []
        for k in range(per):
            start = pl.multiple_of((core ^ relative[b * per + k]) * SHARE, SHARE)
            at = pl.ds(start, SHARE)
            down = jnp.concatenate([down_ref[at, :]] * (n // 128), axis=1)
            weights.append(jnp.exp2(t_ref[at, :] + down + across).astype(jnp.bfloat16))
        w = jnp.concatenate(weights, axis=0)
        denom = jnp.sum(w.astype(jnp.float32), axis=1, keepdims=True)
        numer = dot_nn(w, y)
        for k in range(per):
            part, chunk = slice(k * SHARE, (k + 1) * SHARE), b * per + k
            out_ref[chunk, 0:SHARE, :] = numer[part, 0:128]
            out_ref[chunk, SHARE : 2 * SHARE, :] = numer[part, 128:256]
            out_ref[chunk, 2 * SHARE : CHUNK, :] = jnp.broadcast_to(on_diagonal(denom[part]), (CHUNK - 2 * SHARE, 128))


def project_sent(
    log_m, log_n, relative, t_ref, y_ref, phi_ref, gamma_ref, got_ref, core_ref, out_ref, new_ref, down_ref
):
    total = sum_received(got_ref)
    new_ref[...] = gamma_ref[...] + log_m - log_n - EPS * jnp.log(total[:, 0 : new_ref.shape[1]])
    weighted_sums(log_n, relative, t_ref, y_ref, phi_ref, new_ref, core_ref, out_ref, down_ref)


def project_kept(log_n, relative, t_ref, y_ref, phi_ref, gamma_ref, core_ref, out_ref, down_ref):
    weighted_sums(log_n, relative, t_ref, y_ref, phi_ref, gamma_ref, core_ref, out_ref, down_ref)


def finish(others, got_ref, phi_ref, gamma_ref, sqx_ref, sqy_ref, columns_ref, out_ref, value_ref, potential_ref):
    total = sum_received(got_ref)
    denom = on_diagonal(total[2 * SHARE : 2 * SHARE + 1])
    out_ref[:, 0:128] = total[0:SHARE] / denom
    out_ref[:, 128:256] = total[SHARE : 2 * SHARE] / denom
    n = gamma_ref.shape[1]
    potential_ref[...] = gamma_ref[...] + sqy_ref[...]
    dual = phi_ref[...] + sqx_ref[...]
    dual_sum = tree([columns_ref[k, :, n : n + 1] for k in range(columns_ref.shape[0])], jnp.add)
    value_ref[...] = dual - (dual_sum - dual) / others


def call(body, outs, args, scratch=(), smem=(), anywhere=(), flops=0, limit=40):
    vmem = pl.BlockSpec(memory_space=pltpu.VMEM)
    specs = [vmem for _ in args]
    for k in smem:
        specs[k] = pl.BlockSpec(memory_space=pltpu.SMEM)
    for k in anywhere:
        specs[k] = pl.BlockSpec(memory_space=pl.ANY)
    outs = [s if hasattr(s, "dtype") else jax.ShapeDtypeStruct(s, jnp.float32) for s in outs]
    return pl.pallas_call(
        body,
        out_shape=outs,
        in_specs=specs,
        out_specs=[vmem for _ in outs],
        scratch_shapes=list(scratch),
        compiler_params=pltpu.CompilerParams(vmem_limit_bytes=int(limit * 2**20)),
        cost_estimate=pl.CostEstimate(flops=flops, bytes_accessed=2**20, transcendentals=flops // 512),
    )(*args)


def exchange(x, axis, groups=None):
    return lax.all_to_all(x, axis, 0, 0, axis_index_groups=groups, tiled=True)


def on_device(train_embed, train_label, target_embed, target_label, label_cost):
    m_dev, width = train_embed.shape
    n_dev = target_embed.shape[0]
    trains = lax.axis_size("train")
    targets = lax.axis_size("target")
    log_m = EPS * math.log(m_dev * trains)
    log_n = EPS * math.log(n_dev * targets)
    data = (
        train_embed,
        target_embed,
        train_label.reshape(1, m_dev),
        target_label.reshape(1, n_dev),
        label_cost,
    )
    row_m, row_n = (1, m_dev), (1, n_dev)
    tile_m, tile_n = (m_dev // 128, 128), (n_dev // 128, 128)
    flops = 2 * m_dev * n_dev * 512

    def run(body, outs, tile, *args):
        return call(body, outs, args, scratch=[pltpu.VMEM(tile, jnp.float32)], flops=flops)

    core = (lax.axis_index("target").astype(jnp.int32) & 1).reshape(1)
    local, sqx, sqy = call(
        rows_first,
        [(targets,) + tile_m, row_m, row_n],
        (*data, core),
        scratch=[pltpu.VMEM(tile_m, jnp.float32)]
        + [pltpu.VMEM(v.shape, v.dtype) for v in data]
        + [pltpu.SemaphoreType.DMA((len(data),))],
        anywhere=range(len(data)),
        smem=(len(data),),
        flops=flops,
        limit=54,
    )
    got = exchange(local, "target")
    t, local, phi = run(
        functools.partial(columns_first, log_m), [(m_dev, n_dev), (trains,) + tile_n, row_m], tile_n, *data, got
    )
    got = exchange(local, "train")
    local, gamma = run(functools.partial(rows_next, log_n), [(targets,) + tile_m, row_n], tile_m, t, phi, got)
    got = exchange(local, "target")
    row_more = (1, n_dev + 128)
    local, phi = run(
        functools.partial(columns_next, log_m, log_n), [(trains,) + row_more, row_m], row_more, t, phi, gamma, sqx, got
    )
    columns = exchange(local, "train")

    half = targets // 2
    scratch = [pltpu.VMEM((m_dev, 128), jnp.float32)]
    chunks = (half, CHUNK, 128)
    sent, gamma = call(
        functools.partial(project_sent, log_m, log_n, [2 * k + 1 for k in range(half)]),
        [chunks, row_n],
        (t, target_embed, phi, gamma, columns, core),
        scratch=scratch, smem=(5,), flops=flops,
    )
    sent = lax.ppermute(sent, "target", [(t, t ^ 1) for t in range(targets)])
    (kept,) = call(
        functools.partial(project_kept, log_n, [2 * k for k in range(half)]),
        [chunks],
        (t, target_embed, phi, gamma, core),
        scratch=scratch, smem=(4,), flops=flops,
    )
    groups = [[c + 2 * k for k in range(half)] for c in range(2)]
    got = exchange(kept + sent, "target", groups)
    barycentre, value, potential = call(
        functools.partial(finish, m_dev * trains - 1),
        [(SHARE, width), row_m, row_n],
        (got, phi, gamma, sqx, sqy, columns),
    )
    return (value.reshape(m_dev), potential.reshape(n_dev), barycentre)


def solution(mesh):
    return jax.shard_map(
        on_device,
        mesh=mesh,
        in_specs=(P("train", None), P("train"), P("target", None), P("target"), P()),
        out_specs=(P("train"), P("target"), P(("train", "target"), None)),
        check_vma=False,
    )
```

profile of v0, /device:TPU:1, one launch (start us, length us, event | category | flops | bytes accessed | tf_op | source)
XLA Modules:
  0.0 102.0 jit_solution(9231749325863110545)
XLA Ops:
  0.6 0.0 copy-start
  0.6 0.0 copy-start.6
  0.7 0.0 copy-start.3
  0.7 0.0 copy-start.5
  0.7 0.0 copy-start.4
  0.7 4.0 %shard_map.76 = (f32[32,8,128]{2,1,0:T(8,128)}, f32[1,1024]{1,0:T(1,128)}, f32[1,1024]{1,0:T(1,128)}) custom-call(bf16[1024,256]{1,0:T(8,128)(2,1)} %x_ref.1, bf16[1024,256]{1,0:T(8,128)(2,1)} %y_ref.5, s32[1,1024]{1,0:T(1,128)} %bitcast.5, s32[1,1024]{1,0:T(1,128)} %bitcast.7, f32[8,8]{1,0:T(8,128)} %lc_ref.1, s32[1]{0:T(128)} %bitcast.2.core_ref), custom_call_target="tpu_custom_call" | custom-call | flops 1073741824 | bytes 1048576 | tf_op jit(solution)/shard_map/pallas_call | solution.py:265
  4.7 22.2 %all_to_all.25.got_ref = f32[32,8,128]{2,1,0:T(8,128)S(1)} all-to-all(f32[32,8,128]{2,1,0:T(8,128)} %get-tuple-element.18), channel_id=1, replica_groups=mesh['train'=16,'target'=32] {'target'}, dimensions={0} | all-to-all | bytes 262144 | tf_op jit(solution)/shard_map/all_to_all | solution.py:277
  26.8 0.0 copy-done
  26.8 0.0 copy-done.6
  26.8 0.0 copy-done.3
  26.9 0.0 copy-done.5
  26.9 0.0 copy-done.4
  26.9 0.0 copy-start.1
  26.9 1.9 %shard_map.77 = (f32[1024,1024]{1,0:T(8,128)S(1)}, f32[16,8,128]{2,1,0:T(8,128)S(1)}, f32[1,1024]{1,0:T(1,128)S(1)}) custom-call(bf16[1024,256]{1,0:T(8,128)(2,1)S(1)} %copy-done.3, bf16[1024,256]{1,0:T(8,128)(2,1)S(1)} %copy-done, s32[1,1024]{1,0:T(1,128)S(1)} %bitcast.6, s32[1,1024]{1,0:T(1,128)S(1)} %bitcast.8, f32[8,8]{1,0:T(8,128)S(1)} %copy-done.6, ...), custom_call_target="tpu_custom_call" | custom-call | flops 1073741824 | bytes 1048576 | tf_op jit(solution)/shard_map/pallas_call | solution.py:265
  28.8 17.8 %all_to_all.26.got_ref = f32[16,8,128]{2,1,0:T(8,128)S(1)} all-to-all(f32[16,8,128]{2,1,0:T(8,128)S(1)} %get-tuple-element.21), channel_id=1, replica_groups=mesh['train'=16,'target'=32] {'train'}, dimensions={0} | all-to-all | bytes 131072 | tf_op jit(solution)/shard_map/all_to_all | solution.py:277
  46.6 0.7 shard_map.78
  47.3 14.1 %all_to_all.27.got_ref = f32[32,8,128]{2,1,0:T(8,128)S(1)} all-to-all(f32[32,8,128]{2,1,0:T(8,128)S(1)} %get-tuple-element.24), channel_id=1, replica_groups=mesh['train'=16,'target'=32] {'target'}, dimensions={0} | all-to-all | bytes 262144 | tf_op jit(solution)/shard_map/all_to_all | solution.py:277
  61.4 0.0 copy-done.1
  61.4 0.7 shard_map.79
  62.1 11.5 %all_to_all.28.got_ref.columns_ref = f32[16,1,1152]{2,1,0:T(1,128)S(1)} all-to-all(f32[16,1,1152]{2,1,0:T(1,128)S(1)} %get-tuple-element.26), channel_id=1, replica_groups=mesh['train'=16,'target'=32] {'train'}, dimensions={0} | all-to-all | bytes 147456 | tf_op jit(solution)/shard_map/all_to_all | solution.py:277
  73.6 0.9 shard_map.80
  74.5 0.0 copy-start.2
  74.5 3.6 %collective-permute-start = (f32[16,72,128]{2,1,0:T(8,128)S(1)}, f32[16,72,128]{2,1,0:T(8,128)S(1)}, u32[]{:S(2)}, u32[]{:S(2)}) collective-permute-start(f32[16,72,128]{2,1,0:T(8,128)S(1)} %get-tuple-element.28), channel_id=1, source_target_pairs={{0,1},{1,0},{2,3},{3,2},{4,5},{5,4},{6,7},{7,6},{8,9},{9,8},{10,11... | collective-permute-start | bytes 1769480 | tf_op jit(solution)/shard_map/ppermute | solution.py:336
  78.1 0.9 shard_map.81
  79.0 0.7 collective-permute-done
  79.7 0.1 add.3
  79.8 21.5 %all_to_all.29.got_ref = f32[16,72,128]{2,1,0:T(8,128)S(1)} all-to-all(f32[16,72,128]{2,1,0:T(8,128)S(1)} %add.3), channel_id=1, replica_groups={{0,2,4,6,8,10,12,14,16,18,20,22,24,26,28,30},{1,3,5,7,9,11,13,15,17,19,..., dimensions={0} | all-to-all | bytes 1179648 | tf_op jit(solution)/shard_map/all_to_all | solution.py:277
  101.3 0.0 copy-done.2
  101.3 0.7 shard_map.82
Async XLA Ops:
  0.6 26.2 %copy-start = (bf16[1024,256]{1,0:T(8,128)(2,1)S(1)}, bf16[1024,256]{1,0:T(8,128)(2,1)}, u32[]{:S(2)}) copy-start(bf16[1024,256]{1,0:T(8,128)(2,1)} %y_ref.5) | copy-start | bytes 1572868
  0.6 26.2 %copy-start.6 = (f32[8,8]{1,0:T(8,128)S(1)}, f32[8,8]{1,0:T(8,128)}, u32[]{:S(2)}) copy-start(f32[8,8]{1,0:T(8,128)} %lc_ref.1) | copy-start | bytes 772
  0.7 26.2 %copy-start.3 = (bf16[1024,256]{1,0:T(8,128)(2,1)S(1)}, bf16[1024,256]{1,0:T(8,128)(2,1)}, u32[]{:S(2)}) copy-start(bf16[1024,256]{1,0:T(8,128)(2,1)} %x_ref.1) | copy-start | bytes 1572868
  0.7 26.2 %copy-start.5 = (s32[1024]{0:T(1024)S(1)}, s32[1024]{0:T(1024)}, u32[]{:S(2)}) copy-start(s32[1024]{0:T(1024)} %param.8) | copy-start | bytes 12292
  0.7 26.2 %copy-start.4 = (s32[1024]{0:T(1024)S(1)}, s32[1024]{0:T(1024)}, u32[]{:S(2)}) copy-start(s32[1024]{0:T(1024)} %param.6) | copy-start | bytes 12292
  26.9 34.6 %copy-start.1 = (f32[1,1024]{1,0:T(1,128)S(1)}, f32[1,1024]{1,0:T(1,128)}, u32[]{:S(2)}) copy-start(f32[1,1024]{1,0:T(1,128)} %get-tuple-element.23.sqx_ref) | copy-start | bytes 12292
  74.5 26.8 %copy-start.2 = (f32[1,1024]{1,0:T(1,128)S(1)}, f32[1,1024]{1,0:T(1,128)}, u32[]{:S(2)}) copy-start(f32[1,1024]{1,0:T(1,128)} %get-tuple-element.29.sqy_ref) | copy-start | bytes 12292
  74.5 5.2 %collective-permute-start = (f32[16,72,128]{2,1,0:T(8,128)S(1)}, f32[16,72,128]{2,1,0:T(8,128)S(1)}, u32[]{:S(2)}, u32[]{:S(2)}) collective-permute-start(f32[16,72,128]{2,1,0:T(8,128)S(1)} %get-tuple-element.28), channel_id=1, source_target_pairs={{0,1},{1,0},{2,3},{3,2},{4,5},{5,4},{6,7},{7,6},{8,9},{9,8},{10,11... | collective-permute-start | bytes 1769480 | tf_op jit(solution)/shard_map/ppermute | solution.py:336
where the time goes:
time: 102 us
  blocking collectives  87 us (85%)
  Pallas kernels  9.87 us (10%)
  starting transfers between devices  3.56 us (3%)
    all_to_all x5, blocking collectives, exchange(): return lax.all_to_all(x, axis, 0, 0, axis_index_groups=groups, tiled=True)  87 us
    pallas_call x7, Pallas kernels, call(): pl.pallas_call(body, out_shape=outs, in_specs=specs, out_specs=[vmem for...  9.87 us
    ppermute x1, starting transfers between devices, on_device(): sent = lax.ppermute(sent, 'target', [(t, t ^ 1) for t in range(targets)])  3.56 us
  transfers between devices with their start and end apart: 1, of which 1 were waited for; matrix products, arithmetic and copies ran while one was open for 0% of the time, Pallas kernels for 1%

commit v1 on v0

--- a/solution.py
+++ b/solution.py
@@ -92,11 +92,14 @@
     return parts[0]
 
 
-def lse_received(ref):
-    parts = [ref[k] for k in range(ref.shape[0])]
+def lse(parts):
     top = tree(parts, jnp.maximum)
     total = tree([jnp.exp((part - top) * (1.0 / EPS)) for part in parts], jnp.add)
-    return in_lanes(top + EPS * jnp.log(total))
+    return top + EPS * jnp.log(total)
+
+
+def lse_received(ref):
+    return in_lanes(lse([ref[k] for k in range(ref.shape[0])]))
 
 
 def sum_received(ref):
@@ -117,7 +120,7 @@
 
 def rows_first(
     x_any, y_any, lx_any, ly_any, lc_any, core_ref,
-    out_ref, sqx_ref, sqy_ref, at_ref, x_ref, y_ref, lx_ref, ly_ref, lc_ref, sems,
+    wide_any, out_ref, sqx_ref, sqy_ref, at_ref, x_ref, y_ref, lx_ref, ly_ref, lc_ref, wide_ref, sems,
 ):
     pairs = [(ly_any, ly_ref), (lc_any, lc_ref), (lx_any, lx_ref), (y_any, y_ref), (x_any, x_ref)]
     copies = fetch(pairs, sems)
@@ -126,6 +129,14 @@
     columns = as_columns(target_rows(ly_ref[...], jnp.zeros(ly_ref.shape, jnp.float32), lc_ref[...]))
     copies[3].wait()
     y = y_ref[...]
+    n, width = y.shape
+    wide_ref[0:n, :] = y.astype(jnp.float32)
+    wide_ref[n : n + 8, :] = jnp.zeros((8, width), jnp.float32)
+    label = ly_ref[...].astype(jnp.float32)
+    for k in range(n // width):
+        wide_ref[n + k : n + k + 1, :] = label[:, k * width : (k + 1) * width]
+    wide = pltpu.make_async_copy(wide_ref, wide_any, sems.at[len(pairs)])
+    wide.start()
     means = square_means(y)
     norms = jnp.concatenate([means * SCALE] * (LANES // 128), axis=1)
     copies[4].wait()
@@ -141,6 +152,7 @@
     sqx_ref[...] = square_means(x_ref[...]).T[0:1]
     sqy_ref[...] = means.T[0:1]
     to_everyone(at_ref[...], out_ref)
+    wide.wait()
 
 
 def in_rows(v):
@@ -194,6 +206,7 @@
     for k in range(n // 128):
         at = slice(k * 128, (k + 1) * 128)
         at_ref[:, at] = jnp.sum(jnp.exp2(t_ref[:, at] + down + across[:, at]), axis=0, keepdims=True)
+    at_ref[:, 0:n] = EPS * jnp.log(at_ref[:, 0:n]) - (gamma_ref[...] + log_m)
     dual_sum = jnp.sum(phi + sqx_ref[...], axis=1, keepdims=True)
     at_ref[:, n : n + 128] = jnp.broadcast_to(dual_sum, (1, 128))
     to_everyone(at_ref[...], out_ref)
@@ -206,40 +219,45 @@
     return jnp.sum(jnp.where(row == column, v, 0.0), axis=axis, keepdims=True)
 
 
-def weighted_sums(shift, relative, t_ref, y_ref, phi_ref, gamma_ref, core_ref, out_ref, down_ref):
+def project(
+    log_n, t_ref, x_ref, y_ref, lx_ref, lc_ref, wide_ref, phi_ref, got_ref, core_ref,
+    out_ref, gamma_ref, down_ref, aug_ref, xs_ref, xa_ref,
+):
     core = core_ref[0]
-    n = t_ref.shape[1]
-    down_ref[...] = in_rows((phi_ref[...] + shift) * LOG2)
-    across = gamma_ref[...] * LOG2
+    n, width = y_ref.shape
+    half = got_ref.shape[0] // 2
+    first, second = (-log_n - lse([got_ref[half * p + k, :, 0:n] for k in range(half)]) for p in range(2))
+    mine = jnp.where(core == 0, first, second)
+    other = jnp.where(core == 0, second, first)
+    gamma_ref[...] = mine
+    across = mine * LOG2
+    down_ref[...] = in_rows((phi_ref[...] + log_n) * LOG2)
+    aug_ref[...] = as_columns(train_rows(lx_ref[...], jnp.zeros(lx_ref.shape, jnp.float32))).astype(jnp.float32)
     y = y_ref[...]
-    per = min(8, len(relative))
-    for b in range(len(relative) // per):
-        weights = []
+    y_other = wide_ref[0:n, :].astype(jnp.bfloat16)
+    rows = as_rows(target_rows(in_lanes(wide_ref[n : n + n // width, :]), other, lc_ref[...]))
+    chunks = out_ref.shape[0]
+    per = min(8, chunks)
+    for b in range(chunks // per):
+        weights, downs = [], []
         for k in range(per):
-            start = pl.multiple_of((core ^ relative[b * per + k]) * SHARE, SHARE)
-            at = pl.ds(start, SHARE)
-            down = jnp.concatenate([down_ref[at, :]] * (n // 128), axis=1)
-            weights.append(jnp.exp2(t_ref[at, :] + down + across).astype(jnp.bfloat16))
+            start = pl.multiple_of((2 * (b * per + k) + core) * SHARE, SHARE)
+            at, to = pl.ds(start, SHARE), pl.ds((b * per + k) * SHARE, SHARE)
+            xs_ref[to, :] = x_ref[at, :]
+            xa_ref[to, :] = aug_ref[at, :].astype(jnp.bfloat16)
+            downs.append(jnp.concatenate([down_ref[at, :]] * (n // 128), axis=1))
+            weights.append(jnp.exp2(t_ref[at, :] + downs[k] + across).astype(jnp.bfloat16))
         w = jnp.concatenate(weights, axis=0)
-        denom = jnp.sum(w.astype(jnp.float32), axis=1, keepdims=True)
-        numer = dot_nn(w, y)
+        block = pl.ds(b * per * SHARE, per * SHARE)
+        t = dot_nt(xs_ref[block, :], y_other) + dot_nn(xa_ref[block, :], rows)
+        v = jnp.exp2(t * KAPPA + jnp.concatenate(downs, axis=0)).astype(jnp.bfloat16)
+        denom = jnp.sum(w.astype(jnp.float32) + v.astype(jnp.float32), axis=1, keepdims=True)
+        numer = dot_nn(w, y) + dot_nn(v, y_other)
         for k in range(per):
             part, chunk = slice(k * SHARE, (k + 1) * SHARE), b * per + k
             out_ref[chunk, 0:SHARE, :] = numer[part, 0:128]
             out_ref[chunk, SHARE : 2 * SHARE, :] = numer[part, 128:256]
             out_ref[chunk, 2 * SHARE : CHUNK, :] = jnp.broadcast_to(on_diagonal(denom[part]), (CHUNK - 2 * SHARE, 128))
-
-
-def project_sent(
-    log_m, log_n, relative, t_ref, y_ref, phi_ref, gamma_ref, got_ref, core_ref, out_ref, new_ref, down_ref
-):
-    total = sum_received(got_ref)
-    new_ref[...] = gamma_ref[...] + log_m - log_n - EPS * jnp.log(total[:, 0 : new_ref.shape[1]])
-    weighted_sums(log_n, relative, t_ref, y_ref, phi_ref, new_ref, core_ref, out_ref, down_ref)
-
-
-def project_kept(log_n, relative, t_ref, y_ref, phi_ref, gamma_ref, core_ref, out_ref, down_ref):
-    weighted_sums(log_n, relative, t_ref, y_ref, phi_ref, gamma_ref, core_ref, out_ref, down_ref)
 
 
 def finish(others, got_ref, phi_ref, gamma_ref, sqx_ref, sqy_ref, columns_ref, out_ref, value_ref, potential_ref):
@@ -250,23 +268,24 @@
     n = gamma_ref.shape[1]
     potential_ref[...] = gamma_ref[...] + sqy_ref[...]
     dual = phi_ref[...] + sqx_ref[...]
-    dual_sum = tree([columns_ref[k, :, n : n + 1] for k in range(columns_ref.shape[0])], jnp.add)
+    dual_sum = tree([columns_ref[k, :, n : n + 1] for k in range(columns_ref.shape[0] // 2)], jnp.add)
     value_ref[...] = dual - (dual_sum - dual) / others
 
 
-def call(body, outs, args, scratch=(), smem=(), anywhere=(), flops=0, limit=40):
+def call(body, outs, args, scratch=(), smem=(), anywhere=(), anywhere_out=(), flops=0, limit=40):
     vmem = pl.BlockSpec(memory_space=pltpu.VMEM)
     specs = [vmem for _ in args]
     for k in smem:
         specs[k] = pl.BlockSpec(memory_space=pltpu.SMEM)
     for k in anywhere:
         specs[k] = pl.BlockSpec(memory_space=pl.ANY)
+    out_specs = [pl.BlockSpec(memory_space=pl.ANY) if k in anywhere_out else vmem for k in range(len(outs))]
     outs = [s if hasattr(s, "dtype") else jax.ShapeDtypeStruct(s, jnp.float32) for s in outs]
     return pl.pallas_call(
         body,
         out_shape=outs,
         in_specs=specs,
-        out_specs=[vmem for _ in outs],
+        out_specs=out_specs,
         scratch_shapes=list(scratch),
         compiler_params=pltpu.CompilerParams(vmem_limit_bytes=int(limit * 2**20)),
         cost_estimate=pl.CostEstimate(flops=flops, bytes_accessed=2**20, transcendentals=flops // 512),
@@ -299,18 +318,21 @@
         return call(body, outs, args, scratch=[pltpu.VMEM(tile, jnp.float32)], flops=flops)
 
     core = (lax.axis_index("target").astype(jnp.int32) & 1).reshape(1)
-    local, sqx, sqy = call(
+    wide_shape = (n_dev + 8, width)
+    wide, local, sqx, sqy = call(
         rows_first,
-        [(targets,) + tile_m, row_m, row_n],
+        [wide_shape, (targets,) + tile_m, row_m, row_n],
         (*data, core),
         scratch=[pltpu.VMEM(tile_m, jnp.float32)]
         + [pltpu.VMEM(v.shape, v.dtype) for v in data]
-        + [pltpu.SemaphoreType.DMA((len(data),))],
+        + [pltpu.VMEM(wide_shape, jnp.float32), pltpu.SemaphoreType.DMA((len(data) + 1,))],
         anywhere=range(len(data)),
+        anywhere_out=(0,),
         smem=(len(data),),
         flops=flops,
         limit=54,
     )
+    wide = lax.ppermute(wide, "target", [(k, k ^ 1) for k in range(targets)])
     got = exchange(local, "target")
     t, local, phi = run(
         functools.partial(columns_first, log_m), [(m_dev, n_dev), (trains,) + tile_n, row_m], tile_n, *data, got
@@ -320,28 +342,28 @@
     got = exchange(local, "target")
     row_more = (1, n_dev + 128)
     local, phi = run(
-        functools.partial(columns_next, log_m, log_n), [(trains,) + row_more, row_m], row_more, t, phi, gamma, sqx, got
-    )
-    columns = exchange(local, "train")
+        functools.partial(columns_next, log_m, log_n), [(2 * trains,) + row_more, row_m], row_more, t, phi, gamma, sqx, got
+    )
+    chips = [
+        [a * targets + 2 * k + c for c in range(2) for a in range(trains)] for k in range(targets // 2)
+    ]
+    columns = exchange(local, ("train", "target"), chips)
 
     half = targets // 2
-    scratch = [pltpu.VMEM((m_dev, 128), jnp.float32)]
-    chunks = (half, CHUNK, 128)
-    sent, gamma = call(
-        functools.partial(project_sent, log_m, log_n, [2 * k + 1 for k in range(half)]),
-        [chunks, row_n],
-        (t, target_embed, phi, gamma, columns, core),
-        scratch=scratch, smem=(5,), flops=flops,
-    )
-    sent = lax.ppermute(sent, "target", [(t, t ^ 1) for t in range(targets)])
-    (kept,) = call(
-        functools.partial(project_kept, log_n, [2 * k for k in range(half)]),
-        [chunks],
-        (t, target_embed, phi, gamma, core),
-        scratch=scratch, smem=(4,), flops=flops,
-    )
-    groups = [[c + 2 * k for k in range(half)] for c in range(2)]
-    got = exchange(kept + sent, "target", groups)
+    got, gamma = call(
+        functools.partial(project, log_n),
+        [(half, CHUNK, 128), row_n],
+        (t, train_embed, target_embed, data[2], label_cost, wide, phi, columns, core),
+        scratch=[
+            pltpu.VMEM((m_dev, 128), jnp.float32),
+            pltpu.VMEM((m_dev, 128), jnp.float32),
+            pltpu.VMEM((SHARE * half, width), jnp.bfloat16),
+            pltpu.VMEM((SHARE * half, 128), jnp.bfloat16),
+        ],
+        smem=(8,),
+        flops=flops,
+    )
+    got = exchange(got, "target", [[c + 2 * k for k in range(half)] for c in range(2)])
     barycentre, value, potential = call(
         functools.partial(finish, m_dev * trains - 1),
         [(SHARE, width), row_m, row_n],

time: 102 us -> 101 us (level)
  the two profiles are of different devices: /device:TPU:1 before, /device:TPU:8 now
where the time goes in v1:
time: 101 us
  blocking collectives  68.2 us (68%)
  starting transfers between devices  13.8 us (14%)
  Pallas kernels  10.4 us (10%)
  waiting for transfers between devices  7.42 us (7%)
    all_to_all x4, blocking collectives, exchange(): return lax.all_to_all(x, axis, 0, 0, axis_index_groups=groups, tiled=True)  68.2 us
    all_to_all x1, starting transfers between devices, exchange(): return lax.all_to_all(x, axis, 0, 0, axis_index_groups=groups, tiled=True)  11.6 us
    pallas_call x6, Pallas kernels, call(): pl.pallas_call(body, out_shape=outs, in_specs=specs, out_specs=out_specs,...  10.4 us
    all_to_all x1, waiting for transfers between devices, exchange(): return lax.all_to_all(x, axis, 0, 0, axis_index_groups=groups, tiled=True)  7.42 us
    ppermute x1, starting transfers between devices, on_device(): wide = lax.ppermute(wide, 'target', [(k, k ^ 1) for k in range(targets)])  2.18 us
  transfers between devices with their start and end apart: 2, of which 1 were waited for; matrix products, arithmetic and copies ran while one was open for 0% of the time, Pallas kernels for 4%

profile of v1, /device:TPU:8, one launch (start us, length us, event | category | flops | bytes accessed | tf_op | source)
XLA Modules:
  0.0 100.6 jit_solution(11695852808305266754)
XLA Ops:
  0.6 0.0 copy-start
  0.6 0.0 copy-start.1
  0.7 0.0 copy-start.4
  0.7 0.0 copy-start.5
  0.7 0.0 copy-start.6
  0.7 4.0 %shard_map.76 = (f32[1032,256]{1,0:T(8,128)}, f32[32,8,128]{2,1,0:T(8,128)}, f32[1,1024]{1,0:T(1,128)}, f32[1,1024]{1,0:T(1,128)}) custom-call(bf16[1024,256]{1,0:T(8,128)(2,1)} %x_ref.3, bf16[1024,256]{1,0:T(8,128)(2,1)} %y_ref.3, s32[1,1024]{1,0:T(1,128)} %bitcast.5, s32[1,1024]{1,0:T(1,128)} %bitcast.8, f32[8,8]{1,0:T(8,128)} %lc_ref.3, s32[1]{0:T(128)} %bitcast.2.core_ref), custom_call_target="tpu_custom_call" | custom-call | flops 1073741824 | bytes 1048576 | tf_op jit(solution)/shard_map/pallas_call | solution.py:284
  4.7 11.6 %all-to-all-start = ((f32[32,8,128]{2,1,0:T(8,128)}), f32[32,8,128]{2,1,0:T(8,128)S(1)}, u32[]{:S(2)}, u32[]{:S(2)}) async-start(f32[32,8,128]{2,1,0:T(8,128)} %get-tuple-element.19), calls=%async_computation | async-start | bytes 262144 | tf_op jit(solution)/shard_map/all_to_all | solution.py:296
  16.4 2.2 %collective-permute-start = (f32[1032,256]{1,0:T(8,128)}, f32[1032,256]{1,0:T(8,128)S(1)}, u32[]{:S(2)}, u32[]{:S(2)}) collective-permute-start(f32[1032,256]{1,0:T(8,128)} %get-tuple-element.21), channel_id=1, source_target_pairs={{0,1},{1,0},{2,3},{3,2},{4,5},{5,4},{6,7},{7,6},{8,9},{9,8},{10,11... | collective-permute-start | bytes 3170312 | tf_op jit(solution)/shard_map/ppermute | solution.py:335
  18.6 7.4 %all-to-all-done.got_ref = f32[32,8,128]{2,1,0:T(8,128)S(1)} async-done(((f32[32,8,128]{2,1,0:T(8,128)}), f32[32,8,128]{2,1,0:T(8,128)S(1)}, u32[]{:S(2)}, u32[]{:S(2)}) %all-to-all-start) | async-done | bytes 131104 | tf_op jit(solution)/shard_map/all_to_all | solution.py:296
  26.0 0.0 copy-done
  26.0 0.0 copy-done.1
  26.0 0.0 copy-done.4
  26.0 0.0 copy-done.5
  26.0 0.0 copy-done.6
  26.0 2.0 %shard_map.77 = (f32[1024,1024]{1,0:T(8,128)S(1)}, f32[16,8,128]{2,1,0:T(8,128)S(1)}, f32[1,1024]{1,0:T(1,128)S(1)}) custom-call(bf16[1024,256]{1,0:T(8,128)(2,1)S(1)} %copy-done, bf16[1024,256]{1,0:T(8,128)(2,1)S(1)} %copy-done.1, s32[1,1024]{1,0:T(1,128)S(1)} %bitcast.6, s32[1,1024]{1,0:T(1,128)S(1)} %bitcast.9, f32[8,8]{1,0:T(8,128)S(1)} %copy-done.5, ...), custom_call_target="tpu_custom_call" | custom-call | flops 1073741824 | bytes 1048576 | tf_op jit(solution)/shard_map/pallas_call | solution.py:284
  28.0 18.5 %all_to_all.25.got_ref = f32[16,8,128]{2,1,0:T(8,128)S(1)} all-to-all(f32[16,8,128]{2,1,0:T(8,128)S(1)} %get-tuple-element.23), channel_id=1, replica_groups=mesh['train'=16,'target'=32] {'train'}, dimensions={0} | all-to-all | bytes 131072 | tf_op jit(solution)/shard_map/all_to_all | solution.py:296
  46.6 0.0 copy-start.2
  46.6 0.8 shard_map.78
  47.4 12.6 %all_to_all.26.got_ref = f32[32,8,128]{2,1,0:T(8,128)S(1)} all-to-all(f32[32,8,128]{2,1,0:T(8,128)S(1)} %get-tuple-element.26), channel_id=1, replica_groups=mesh['train'=16,'target'=32] {'target'}, dimensions={0} | all-to-all | bytes 262144 | tf_op jit(solution)/shard_map/all_to_all | solution.py:296
  59.9 0.0 copy-done.2
  59.9 0.8 shard_map.79
  60.7 14.8 %all_to_all.27.got_ref.columns_ref = f32[32,1,1152]{2,1,0:T(1,128)S(1)} all-to-all(f32[32,1,1152]{2,1,0:T(1,128)S(1)} %get-tuple-element.28), channel_id=1, replica_groups={{0,32,64,96,128,160,192,224,256,288,320,352,384,416,448,480,1,33,65,97,..., dimensions={0} | all-to-all | bytes 294912 | tf_op jit(solution)/shard_map/all_to_all | solution.py:296
  75.5 0.0 collective-permute-done.wide_ref
  75.5 2.0 %shard_map.80 = (f32[16,72,128]{2,1,0:T(8,128)S(1)}, f32[1,1024]{1,0:T(1,128)S(1)}) custom-call(f32[1024,1024]{1,0:T(8,128)S(1)} %get-tuple-element.20.t_ref, bf16[1024,256]{1,0:T(8,128)(2,1)S(1)} %copy-done, bf16[1024,256]{1,0:T(8,128)(2,1)S(1)} %copy-done.1, s32[1,1024]{1,0:T(1,128)S(1)} %bitcast.7, f32[8,8]{1,0:T(8,128)S(1)} %copy-done.5, ...), custom_call_target="tpu_custom_call" | custom-call | flops 1073741824 | bytes 1048576 | tf_op jit(solution)/shard_map/pallas_call | solution.py:284
  77.6 0.0 copy-start.3
  77.6 22.3 %all_to_all.28.got_ref = f32[16,72,128]{2,1,0:T(8,128)S(1)} all-to-all(f32[16,72,128]{2,1,0:T(8,128)S(1)} %get-tuple-element.29), channel_id=1, replica_groups={{0,2,4,6,8,10,12,14,16,18,20,22,24,26,28,30},{1,3,5,7,9,11,13,15,17,19,..., dimensions={0} | all-to-all | bytes 1179648 | tf_op jit(solution)/shard_map/all_to_all | solution.py:296
  99.8 0.0 copy-done.3
  99.8 0.7 shard_map.81
Async XLA Ops:
  0.6 25.3 %copy-start = (bf16[1024,256]{1,0:T(8,128)(2,1)S(1)}, bf16[1024,256]{1,0:T(8,128)(2,1)}, u32[]{:S(2)}) copy-start(bf16[1024,256]{1,0:T(8,128)(2,1)} %x_ref.3) | copy-start | bytes 1572868
  0.6 25.3 %copy-start.1 = (bf16[1024,256]{1,0:T(8,128)(2,1)S(1)}, bf16[1024,256]{1,0:T(8,128)(2,1)}, u32[]{:S(2)}) copy-start(bf16[1024,256]{1,0:T(8,128)(2,1)} %y_ref.3) | copy-start | bytes 1572868
  0.7 25.3 %copy-start.4 = (s32[1024]{0:T(1024)S(1)}, s32[1024]{0:T(1024)}, u32[]{:S(2)}) copy-start(s32[1024]{0:T(1024)} %param.6) | copy-start | bytes 12292
  0.7 25.3 %copy-start.5 = (f32[8,8]{1,0:T(8,128)S(1)}, f32[8,8]{1,0:T(8,128)}, u32[]{:S(2)}) copy-start(f32[8,8]{1,0:T(8,128)} %lc_ref.3) | copy-start | bytes 772
  0.7 25.3 %copy-start.6 = (s32[1024]{0:T(1024)S(1)}, s32[1024]{0:T(1024)}, u32[]{:S(2)}) copy-start(s32[1024]{0:T(1024)} %param.8) | copy-start | bytes 12292
  4.7 21.3 %all-to-all-start = ((f32[32,8,128]{2,1,0:T(8,128)}), f32[32,8,128]{2,1,0:T(8,128)S(1)}, u32[]{:S(2)}, u32[]{:S(2)}) async-start(f32[32,8,128]{2,1,0:T(8,128)} %get-tuple-element.19), calls=%async_computation | async-start | bytes 262144 | tf_op jit(solution)/shard_map/all_to_all | solution.py:296
  16.4 59.2 %collective-permute-start = (f32[1032,256]{1,0:T(8,128)}, f32[1032,256]{1,0:T(8,128)S(1)}, u32[]{:S(2)}, u32[]{:S(2)}) collective-permute-start(f32[1032,256]{1,0:T(8,128)} %get-tuple-element.21), channel_id=1, source_target_pairs={{0,1},{1,0},{2,3},{3,2},{4,5},{5,4},{6,7},{7,6},{8,9},{9,8},{10,11... | collective-permute-start | bytes 3170312 | tf_op jit(solution)/shard_map/ppermute | solution.py:335
  46.6 13.4 %copy-start.2 = (f32[1,1024]{1,0:T(1,128)S(1)}, f32[1,1024]{1,0:T(1,128)}, u32[]{:S(2)}) copy-start(f32[1,1024]{1,0:T(1,128)} %get-tuple-element.25.sqx_ref) | copy-start | bytes 12292
  77.6 22.3 %copy-start.3 = (f32[1,1024]{1,0:T(1,128)S(1)}, f32[1,1024]{1,0:T(1,128)}, u32[]{:S(2)}) copy-start(f32[1,1024]{1,0:T(1,128)} %get-tuple-element.31.sqy_ref) | copy-start | bytes 12292

commit v2 on v1

--- a/solution.py
+++ b/solution.py
@@ -122,8 +122,9 @@
     x_any, y_any, lx_any, ly_any, lc_any, core_ref,
     wide_any, out_ref, sqx_ref, sqy_ref, at_ref, x_ref, y_ref, lx_ref, ly_ref, lc_ref, wide_ref, sems,
 ):
-    pairs = [(ly_any, ly_ref), (lc_any, lc_ref), (lx_any, lx_ref), (y_any, y_ref), (x_any, x_ref)]
-    copies = fetch(pairs, sems)
+    pairs = [(ly_any, ly_ref), (lc_any, lc_ref), (lx_any, lx_ref), (y_any, y_ref)]
+    steps = [slice(k * LANES, (k + 1) * LANES) for k in range(x_ref.shape[0] // LANES)]
+    copies = fetch(pairs + [(x_any.at[at, :], x_ref.at[at, :]) for at in steps], sems)
     wait_all(copies[:3])
     rows = as_rows(train_rows(lx_ref[...], jnp.zeros(lx_ref.shape, jnp.float32)))
     columns = as_columns(target_rows(ly_ref[...], jnp.zeros(ly_ref.shape, jnp.float32), lc_ref[...]))
@@ -135,13 +136,12 @@
     label = ly_ref[...].astype(jnp.float32)
     for k in range(n // width):
         wide_ref[n + k : n + k + 1, :] = label[:, k * width : (k + 1) * width]
-    wide = pltpu.make_async_copy(wide_ref, wide_any, sems.at[len(pairs)])
+    wide = pltpu.make_async_copy(wide_ref, wide_any, sems.at[len(copies)])
     wide.start()
     means = square_means(y)
     norms = jnp.concatenate([means * SCALE] * (LANES // 128), axis=1)
-    copies[4].wait()
-    for k in range(x_ref.shape[0] // LANES):
-        at = slice(k * LANES, (k + 1) * LANES)
+    for k, at in enumerate(steps):
+        copies[len(pairs) + k].wait()
         t = dot_nt(y, x_ref[at, :]) + dot_nn(columns, rows[:, at]) - norms
         top = jnp.max(t, axis=0, keepdims=True)
         total = jnp.sum(jnp.exp2((t - top) * KAPPA), axis=0, keepdims=True)
@@ -226,7 +226,7 @@
     core = core_ref[0]
     n, width = y_ref.shape
     half = got_ref.shape[0] // 2
-    first, second = (-log_n - lse([got_ref[half * p + k, :, 0:n] for k in range(half)]) for p in range(2))
+    first, second = (-log_n - lse([got_ref[2 * k + p, :, 0:n] for k in range(half)]) for p in range(2))
     mine = jnp.where(core == 0, first, second)
     other = jnp.where(core == 0, second, first)
     gamma_ref[...] = mine
@@ -268,7 +268,7 @@
     n = gamma_ref.shape[1]
     potential_ref[...] = gamma_ref[...] + sqy_ref[...]
     dual = phi_ref[...] + sqx_ref[...]
-    dual_sum = tree([columns_ref[k, :, n : n + 1] for k in range(columns_ref.shape[0] // 2)], jnp.add)
+    dual_sum = tree([columns_ref[2 * k, :, n : n + 1] for k in range(columns_ref.shape[0] // 2)], jnp.add)
     value_ref[...] = dual - (dual_sum - dual) / others
 
 
@@ -325,7 +325,7 @@
         (*data, core),
         scratch=[pltpu.VMEM(tile_m, jnp.float32)]
         + [pltpu.VMEM(v.shape, v.dtype) for v in data]
-        + [pltpu.VMEM(wide_shape, jnp.float32), pltpu.SemaphoreType.DMA((len(data) + 1,))],
+        + [pltpu.VMEM(wide_shape, jnp.float32), pltpu.SemaphoreType.DMA((len(data) + m_dev // LANES,))],
         anywhere=range(len(data)),
         anywhere_out=(0,),
         smem=(len(data),),
@@ -345,7 +345,7 @@
         functools.partial(columns_next, log_m, log_n), [(2 * trains,) + row_more, row_m], row_more, t, phi, gamma, sqx, got
     )
     chips = [
-        [a * targets + 2 * k + c for c in range(2) for a in range(trains)] for k in range(targets // 2)
+        [a * targets + 2 * k + c for a in range(trains) for c in range(2)] for k in range(targets // 2)
     ]
     columns = exchange(local, ("train", "target"), chips)
 

time: 101 us -> 102 us (level)
  the two profiles are of different devices: /device:TPU:8 before, /device:TPU:1 now
where the time goes in v2:
time: 102 us; the launch traced here: 100 us
  blocking collectives  65.3 us (64%)
  starting transfers between devices  15.1 us (15%)
  Pallas kernels  12.2 us (12%)
  waiting for transfers between devices  7.11 us (7%)
    all_to_all x4, blocking collectives, exchange(): return lax.all_to_all(x, axis, 0, 0, axis_index_groups=groups, tiled=True)  65.3 us
    all_to_all x1, starting transfers between devices, exchange(): return lax.all_to_all(x, axis, 0, 0, axis_index_groups=groups, tiled=True)  12.9 us
    pallas_call x6, Pallas kernels, call(): pl.pallas_call(body, out_shape=outs, in_specs=specs, out_specs=out_specs,...  12.2 us
    all_to_all x1, waiting for transfers between devices, exchange(): return lax.all_to_all(x, axis, 0, 0, axis_index_groups=groups, tiled=True)  7.11 us
    ppermute x1, starting transfers between devices, on_device(): wide = lax.ppermute(wide, 'target', [(k, k ^ 1) for k in range(targets)])  2.14 us
  transfers between devices with their start and end apart: 2, of which 1 were waited for; matrix products, arithmetic and copies ran while one was open for 0% of the time, Pallas kernels for 4%

profile of v2, /device:TPU:1, one launch (start us, length us, event | category | flops | bytes accessed | tf_op | source)
XLA Modules:
  0.0 100.4 jit_solution(11573399669478040946)
XLA Ops:
  0.6 0.0 copy-start
  0.6 0.0 copy-start.1
  0.7 0.0 copy-start.4
  0.7 0.0 copy-start.5
  0.7 0.0 copy-start.6
  0.7 5.8 %shard_map.76 = (f32[1032,256]{1,0:T(8,128)}, f32[32,8,128]{2,1,0:T(8,128)}, f32[1,1024]{1,0:T(1,128)}, f32[1,1024]{1,0:T(1,128)}) custom-call(bf16[1024,256]{1,0:T(8,128)(2,1)} %x_ref.3, bf16[1024,256]{1,0:T(8,128)(2,1)} %y_ref.3, s32[1,1024]{1,0:T(1,128)} %bitcast.5, s32[1,1024]{1,0:T(1,128)} %bitcast.8, f32[8,8]{1,0:T(8,128)} %lc_ref.3, s32[1]{0:T(128)} %bitcast.2.core_ref), custom_call_target="tpu_custom_call" | custom-call | flops 1073741824 | bytes 1048576 | tf_op jit(solution)/shard_map/pallas_call | solution.py:284
  6.5 12.9 %all-to-all-start = ((f32[32,8,128]{2,1,0:T(8,128)}), f32[32,8,128]{2,1,0:T(8,128)S(1)}, u32[]{:S(2)}, u32[]{:S(2)}) async-start(f32[32,8,128]{2,1,0:T(8,128)} %get-tuple-element.19), calls=%async_computation | async-start | bytes 262144 | tf_op jit(solution)/shard_map/all_to_all | solution.py:296
  19.4 2.1 %collective-permute-start = (f32[1032,256]{1,0:T(8,128)}, f32[1032,256]{1,0:T(8,128)S(1)}, u32[]{:S(2)}, u32[]{:S(2)}) collective-permute-start(f32[1032,256]{1,0:T(8,128)} %get-tuple-element.21), channel_id=1, source_target_pairs={{0,1},{1,0},{2,3},{3,2},{4,5},{5,4},{6,7},{7,6},{8,9},{9,8},{10,11... | collective-permute-start | bytes 3170312 | tf_op jit(solution)/shard_map/ppermute | solution.py:335
  21.6 7.1 %all-to-all-done.got_ref = f32[32,8,128]{2,1,0:T(8,128)S(1)} async-done(((f32[32,8,128]{2,1,0:T(8,128)}), f32[32,8,128]{2,1,0:T(8,128)S(1)}, u32[]{:S(2)}, u32[]{:S(2)}) %all-to-all-start) | async-done | bytes 131104 | tf_op jit(solution)/shard_map/all_to_all | solution.py:296
  28.7 0.0 copy-done
  28.7 0.0 copy-done.1
  28.7 0.0 copy-done.4
  28.7 0.0 copy-done.5
  28.7 0.0 copy-done.6
  28.7 2.0 %shard_map.77 = (f32[1024,1024]{1,0:T(8,128)S(1)}, f32[16,8,128]{2,1,0:T(8,128)S(1)}, f32[1,1024]{1,0:T(1,128)S(1)}) custom-call(bf16[1024,256]{1,0:T(8,128)(2,1)S(1)} %copy-done, bf16[1024,256]{1,0:T(8,128)(2,1)S(1)} %copy-done.1, s32[1,1024]{1,0:T(1,128)S(1)} %bitcast.6, s32[1,1024]{1,0:T(1,128)S(1)} %bitcast.9, f32[8,8]{1,0:T(8,128)S(1)} %copy-done.5, ...), custom_call_target="tpu_custom_call" | custom-call | flops 1073741824 | bytes 1048576 | tf_op jit(solution)/shard_map/pallas_call | solution.py:284
  30.7 17.8 %all_to_all.25.got_ref = f32[16,8,128]{2,1,0:T(8,128)S(1)} all-to-all(f32[16,8,128]{2,1,0:T(8,128)S(1)} %get-tuple-element.23), channel_id=1, replica_groups=mesh['train'=16,'target'=32] {'train'}, dimensions={0} | all-to-all | bytes 131072 | tf_op jit(solution)/shard_map/all_to_all | solution.py:296
  48.5 0.0 copy-start.2
  48.5 0.8 shard_map.78
  49.3 14.1 %all_to_all.26.got_ref = f32[32,8,128]{2,1,0:T(8,128)S(1)} all-to-all(f32[32,8,128]{2,1,0:T(8,128)S(1)} %get-tuple-element.26), channel_id=1, replica_groups=mesh['train'=16,'target'=32] {'target'}, dimensions={0} | all-to-all | bytes 262144 | tf_op jit(solution)/shard_map/all_to_all | solution.py:296
  63.4 0.0 copy-done.2
  63.4 0.8 shard_map.79
  64.2 14.0 %all_to_all.27.got_ref.columns_ref = f32[32,1,1152]{2,1,0:T(1,128)S(1)} all-to-all(f32[32,1,1152]{2,1,0:T(1,128)S(1)} %get-tuple-element.28), channel_id=1, replica_groups={{0,1,32,33,64,65,96,97,128,129,160,161,192,193,224,225,256,257,288,289,..., dimensions={0} | all-to-all | bytes 294912 | tf_op jit(solution)/shard_map/all_to_all | solution.py:296
  78.2 0.0 collective-permute-done.wide_ref
  78.2 2.0 %shard_map.80 = (f32[16,72,128]{2,1,0:T(8,128)S(1)}, f32[1,1024]{1,0:T(1,128)S(1)}) custom-call(f32[1024,1024]{1,0:T(8,128)S(1)} %get-tuple-element.20.t_ref, bf16[1024,256]{1,0:T(8,128)(2,1)S(1)} %copy-done, bf16[1024,256]{1,0:T(8,128)(2,1)S(1)} %copy-done.1, s32[1,1024]{1,0:T(1,128)S(1)} %bitcast.7, f32[8,8]{1,0:T(8,128)S(1)} %copy-done.5, ...), custom_call_target="tpu_custom_call" | custom-call | flops 1073741824 | bytes 1048576 | tf_op jit(solution)/shard_map/pallas_call | solution.py:284
  80.2 0.0 copy-start.3
  80.2 19.4 %all_to_all.28.got_ref = f32[16,72,128]{2,1,0:T(8,128)S(1)} all-to-all(f32[16,72,128]{2,1,0:T(8,128)S(1)} %get-tuple-element.29), channel_id=1, replica_groups={{0,2,4,6,8,10,12,14,16,18,20,22,24,26,28,30},{1,3,5,7,9,11,13,15,17,19,..., dimensions={0} | all-to-all | bytes 1179648 | tf_op jit(solution)/shard_map/all_to_all | solution.py:296
  99.6 0.0 copy-done.3
  99.6 0.7 shard_map.81
Async XLA Ops:
  0.6 28.1 %copy-start = (bf16[1024,256]{1,0:T(8,128)(2,1)S(1)}, bf16[1024,256]{1,0:T(8,128)(2,1)}, u32[]{:S(2)}) copy-start(bf16[1024,256]{1,0:T(8,128)(2,1)} %x_ref.3) | copy-start | bytes 1572868
  0.6 28.0 %copy-start.1 = (bf16[1024,256]{1,0:T(8,128)(2,1)S(1)}, bf16[1024,256]{1,0:T(8,128)(2,1)}, u32[]{:S(2)}) copy-start(bf16[1024,256]{1,0:T(8,128)(2,1)} %y_ref.3) | copy-start | bytes 1572868
  0.7 28.0 %copy-start.4 = (s32[1024]{0:T(1024)S(1)}, s32[1024]{0:T(1024)}, u32[]{:S(2)}) copy-start(s32[1024]{0:T(1024)} %param.6) | copy-start | bytes 12292
  0.7 28.0 %copy-start.5 = (f32[8,8]{1,0:T(8,128)S(1)}, f32[8,8]{1,0:T(8,128)}, u32[]{:S(2)}) copy-start(f32[8,8]{1,0:T(8,128)} %lc_ref.3) | copy-start | bytes 772
  0.7 28.0 %copy-start.6 = (s32[1024]{0:T(1024)S(1)}, s32[1024]{0:T(1024)}, u32[]{:S(2)}) copy-start(s32[1024]{0:T(1024)} %param.8) | copy-start | bytes 12292
  6.5 22.2 %all-to-all-start = ((f32[32,8,128]{2,1,0:T(8,128)}), f32[32,8,128]{2,1,0:T(8,128)S(1)}, u32[]{:S(2)}, u32[]{:S(2)}) async-start(f32[32,8,128]{2,1,0:T(8,128)} %get-tuple-element.19), calls=%async_computation | async-start | bytes 262144 | tf_op jit(solution)/shard_map/all_to_all | solution.py:296
  19.4 58.8 %collective-permute-start = (f32[1032,256]{1,0:T(8,128)}, f32[1032,256]{1,0:T(8,128)S(1)}, u32[]{:S(2)}, u32[]{:S(2)}) collective-permute-start(f32[1032,256]{1,0:T(8,128)} %get-tuple-element.21), channel_id=1, source_target_pairs={{0,1},{1,0},{2,3},{3,2},{4,5},{5,4},{6,7},{7,6},{8,9},{9,8},{10,11... | collective-permute-start | bytes 3170312 | tf_op jit(solution)/shard_map/ppermute | solution.py:335
  48.5 14.9 %copy-start.2 = (f32[1,1024]{1,0:T(1,128)S(1)}, f32[1,1024]{1,0:T(1,128)}, u32[]{:S(2)}) copy-start(f32[1,1024]{1,0:T(1,128)} %get-tuple-element.25.sqx_ref) | copy-start | bytes 12292
  80.2 19.4 %copy-start.3 = (f32[1,1024]{1,0:T(1,128)S(1)}, f32[1,1024]{1,0:T(1,128)}, u32[]{:S(2)}) copy-start(f32[1,1024]{1,0:T(1,128)} %get-tuple-element.31.sqy_ref) | copy-start | bytes 12292

commit v3 on v1

--- a/solution.py
+++ b/solution.py
@@ -135,11 +135,11 @@
     label = ly_ref[...].astype(jnp.float32)
     for k in range(n // width):
         wide_ref[n + k : n + k + 1, :] = label[:, k * width : (k + 1) * width]
-    wide = pltpu.make_async_copy(wide_ref, wide_any, sems.at[len(pairs)])
+    wide = pltpu.make_async_copy(wide_ref, wide_any, sems.at[len(copies)])
     wide.start()
+    copies[4].wait()
     means = square_means(y)
     norms = jnp.concatenate([means * SCALE] * (LANES // 128), axis=1)
-    copies[4].wait()
     for k in range(x_ref.shape[0] // LANES):
         at = slice(k * LANES, (k + 1) * LANES)
         t = dot_nt(y, x_ref[at, :]) + dot_nn(columns, rows[:, at]) - norms
@@ -226,7 +226,7 @@
     core = core_ref[0]
     n, width = y_ref.shape
     half = got_ref.shape[0] // 2
-    first, second = (-log_n - lse([got_ref[half * p + k, :, 0:n] for k in range(half)]) for p in range(2))
+    first, second = (-log_n - lse([got_ref[2 * k + p, :, 0:n] for k in range(half)]) for p in range(2))
     mine = jnp.where(core == 0, first, second)
     other = jnp.where(core == 0, second, first)
     gamma_ref[...] = mine
@@ -268,7 +268,7 @@
     n = gamma_ref.shape[1]
     potential_ref[...] = gamma_ref[...] + sqy_ref[...]
     dual = phi_ref[...] + sqx_ref[...]
-    dual_sum = tree([columns_ref[k, :, n : n + 1] for k in range(columns_ref.shape[0] // 2)], jnp.add)
+    dual_sum = tree([columns_ref[2 * k, :, n : n + 1] for k in range(columns_ref.shape[0] // 2)], jnp.add)
     value_ref[...] = dual - (dual_sum - dual) / others
 
 
@@ -345,7 +345,7 @@
         functools.partial(columns_next, log_m, log_n), [(2 * trains,) + row_more, row_m], row_more, t, phi, gamma, sqx, got
     )
     chips = [
-        [a * targets + 2 * k + c for c in range(2) for a in range(trains)] for k in range(targets // 2)
+        [a * targets + 2 * k + c for a in range(trains) for c in range(2)] for k in range(targets // 2)
     ]
     columns = exchange(local, ("train", "target"), chips)
 

time: 101 us -> 100 us (0.990)
  the two profiles are of different devices: /device:TPU:8 before, /device:TPU:1 now
where the time goes in v3:
time: 100 us; the launch traced here: 98.6 us
  blocking collectives  65.3 us (65%)
  starting transfers between devices  15.1 us (15%)
  Pallas kernels  10.4 us (10%)
  waiting for transfers between devices  7.11 us (7%)
    all_to_all x4, blocking collectives, exchange(): return lax.all_to_all(x, axis, 0, 0, axis_index_groups=groups, tiled=True)  65.3 us
    all_to_all x1, starting transfers between devices, exchange(): return lax.all_to_all(x, axis, 0, 0, axis_index_groups=groups, tiled=True)  12.9 us
    pallas_call x6, Pallas kernels, call(): pl.pallas_call(body, out_shape=outs, in_specs=specs, out_specs=out_specs,...  10.4 us
    all_to_all x1, waiting for transfers between devices, exchange(): return lax.all_to_all(x, axis, 0, 0, axis_index_groups=groups, tiled=True)  7.11 us
    ppermute x1, starting transfers between devices, on_device(): wide = lax.ppermute(wide, 'target', [(k, k ^ 1) for k in range(targets)])  2.14 us
  transfers between devices with their start and end apart: 2, of which 1 were waited for; matrix products, arithmetic and copies ran while one was open for 0% of the time, Pallas kernels for 4%

profile of v3, /device:TPU:1, one launch (start us, length us, event | category | flops | bytes accessed | tf_op | source)
XLA Modules:
  0.0 98.6 jit_solution(998581858631289498)
XLA Ops:
  0.6 0.0 copy-start
  0.6 0.0 copy-start.1
  0.7 0.0 copy-start.4
  0.7 0.0 copy-start.5
  0.7 0.0 copy-start.6
  0.7 4.0 %shard_map.76 = (f32[1032,256]{1,0:T(8,128)}, f32[32,8,128]{2,1,0:T(8,128)}, f32[1,1024]{1,0:T(1,128)}, f32[1,1024]{1,0:T(1,128)}) custom-call(bf16[1024,256]{1,0:T(8,128)(2,1)} %x_ref.3, bf16[1024,256]{1,0:T(8,128)(2,1)} %y_ref.3, s32[1,1024]{1,0:T(1,128)} %bitcast.5, s32[1,1024]{1,0:T(1,128)} %bitcast.8, f32[8,8]{1,0:T(8,128)} %lc_ref.3, s32[1]{0:T(128)} %bitcast.2.core_ref), custom_call_target="tpu_custom_call" | custom-call | flops 1073741824 | bytes 1048576 | tf_op jit(solution)/shard_map/pallas_call | solution.py:284
  4.7 12.9 %all-to-all-start = ((f32[32,8,128]{2,1,0:T(8,128)}), f32[32,8,128]{2,1,0:T(8,128)S(1)}, u32[]{:S(2)}, u32[]{:S(2)}) async-start(f32[32,8,128]{2,1,0:T(8,128)} %get-tuple-element.19), calls=%async_computation | async-start | bytes 262144 | tf_op jit(solution)/shard_map/all_to_all | solution.py:296
  17.6 2.1 %collective-permute-start = (f32[1032,256]{1,0:T(8,128)}, f32[1032,256]{1,0:T(8,128)S(1)}, u32[]{:S(2)}, u32[]{:S(2)}) collective-permute-start(f32[1032,256]{1,0:T(8,128)} %get-tuple-element.21), channel_id=1, source_target_pairs={{0,1},{1,0},{2,3},{3,2},{4,5},{5,4},{6,7},{7,6},{8,9},{9,8},{10,11... | collective-permute-start | bytes 3170312 | tf_op jit(solution)/shard_map/ppermute | solution.py:335
  19.8 7.1 %all-to-all-done.got_ref = f32[32,8,128]{2,1,0:T(8,128)S(1)} async-done(((f32[32,8,128]{2,1,0:T(8,128)}), f32[32,8,128]{2,1,0:T(8,128)S(1)}, u32[]{:S(2)}, u32[]{:S(2)}) %all-to-all-start) | async-done | bytes 131104 | tf_op jit(solution)/shard_map/all_to_all | solution.py:296
  26.9 0.0 copy-done
  26.9 0.0 copy-done.1
  26.9 0.0 copy-done.4
  26.9 0.0 copy-done.5
  26.9 0.0 copy-done.6
  26.9 2.0 %shard_map.77 = (f32[1024,1024]{1,0:T(8,128)S(1)}, f32[16,8,128]{2,1,0:T(8,128)S(1)}, f32[1,1024]{1,0:T(1,128)S(1)}) custom-call(bf16[1024,256]{1,0:T(8,128)(2,1)S(1)} %copy-done, bf16[1024,256]{1,0:T(8,128)(2,1)S(1)} %copy-done.1, s32[1,1024]{1,0:T(1,128)S(1)} %bitcast.6, s32[1,1024]{1,0:T(1,128)S(1)} %bitcast.9, f32[8,8]{1,0:T(8,128)S(1)} %copy-done.5, ...), custom_call_target="tpu_custom_call" | custom-call | flops 1073741824 | bytes 1048576 | tf_op jit(solution)/shard_map/pallas_call | solution.py:284
  29.0 17.8 %all_to_all.25.got_ref = f32[16,8,128]{2,1,0:T(8,128)S(1)} all-to-all(f32[16,8,128]{2,1,0:T(8,128)S(1)} %get-tuple-element.23), channel_id=1, replica_groups=mesh['train'=16,'target'=32] {'train'}, dimensions={0} | all-to-all | bytes 131072 | tf_op jit(solution)/shard_map/all_to_all | solution.py:296
  46.7 0.0 copy-start.2
  46.7 0.8 shard_map.78
  47.5 14.1 %all_to_all.26.got_ref = f32[32,8,128]{2,1,0:T(8,128)S(1)} all-to-all(f32[32,8,128]{2,1,0:T(8,128)S(1)} %get-tuple-element.26), channel_id=1, replica_groups=mesh['train'=16,'target'=32] {'target'}, dimensions={0} | all-to-all | bytes 262144 | tf_op jit(solution)/shard_map/all_to_all | solution.py:296
  61.6 0.0 copy-done.2
  61.6 0.8 shard_map.79
  62.4 14.0 %all_to_all.27.got_ref.columns_ref = f32[32,1,1152]{2,1,0:T(1,128)S(1)} all-to-all(f32[32,1,1152]{2,1,0:T(1,128)S(1)} %get-tuple-element.28), channel_id=1, replica_groups={{0,1,32,33,64,65,96,97,128,129,160,161,192,193,224,225,256,257,288,289,..., dimensions={0} | all-to-all | bytes 294912 | tf_op jit(solution)/shard_map/all_to_all | solution.py:296
  76.4 0.0 collective-permute-done.wide_ref
  76.4 2.0 %shard_map.80 = (f32[16,72,128]{2,1,0:T(8,128)S(1)}, f32[1,1024]{1,0:T(1,128)S(1)}) custom-call(f32[1024,1024]{1,0:T(8,128)S(1)} %get-tuple-element.20.t_ref, bf16[1024,256]{1,0:T(8,128)(2,1)S(1)} %copy-done, bf16[1024,256]{1,0:T(8,128)(2,1)S(1)} %copy-done.1, s32[1,1024]{1,0:T(1,128)S(1)} %bitcast.7, f32[8,8]{1,0:T(8,128)S(1)} %copy-done.5, ...), custom_call_target="tpu_custom_call" | custom-call | flops 1073741824 | bytes 1048576 | tf_op jit(solution)/shard_map/pallas_call | solution.py:284
  78.4 0.0 copy-start.3
  78.5 19.4 %all_to_all.28.got_ref = f32[16,72,128]{2,1,0:T(8,128)S(1)} all-to-all(f32[16,72,128]{2,1,0:T(8,128)S(1)} %get-tuple-element.29), channel_id=1, replica_groups={{0,2,4,6,8,10,12,14,16,18,20,22,24,26,28,30},{1,3,5,7,9,11,13,15,17,19,..., dimensions={0} | all-to-all | bytes 1179648 | tf_op jit(solution)/shard_map/all_to_all | solution.py:296
  97.8 0.0 copy-done.3
  97.8 0.7 shard_map.81
Async XLA Ops:
  0.6 26.3 %copy-start = (bf16[1024,256]{1,0:T(8,128)(2,1)S(1)}, bf16[1024,256]{1,0:T(8,128)(2,1)}, u32[]{:S(2)}) copy-start(bf16[1024,256]{1,0:T(8,128)(2,1)} %x_ref.3) | copy-start | bytes 1572868
  0.6 26.3 %copy-start.1 = (bf16[1024,256]{1,0:T(8,128)(2,1)S(1)}, bf16[1024,256]{1,0:T(8,128)(2,1)}, u32[]{:S(2)}) copy-start(bf16[1024,256]{1,0:T(8,128)(2,1)} %y_ref.3) | copy-start | bytes 1572868
  0.7 26.3 %copy-start.4 = (s32[1024]{0:T(1024)S(1)}, s32[1024]{0:T(1024)}, u32[]{:S(2)}) copy-start(s32[1024]{0:T(1024)} %param.6) | copy-start | bytes 12292
  0.7 26.3 %copy-start.5 = (f32[8,8]{1,0:T(8,128)S(1)}, f32[8,8]{1,0:T(8,128)}, u32[]{:S(2)}) copy-start(f32[8,8]{1,0:T(8,128)} %lc_ref.3) | copy-start | bytes 772
  0.7 26.3 %copy-start.6 = (s32[1024]{0:T(1024)S(1)}, s32[1024]{0:T(1024)}, u32[]{:S(2)}) copy-start(s32[1024]{0:T(1024)} %param.8) | copy-start | bytes 12292
  4.7 22.2 %all-to-all-start = ((f32[32,8,128]{2,1,0:T(8,128)}), f32[32,8,128]{2,1,0:T(8,128)S(1)}, u32[]{:S(2)}, u32[]{:S(2)}) async-start(f32[32,8,128]{2,1,0:T(8,128)} %get-tuple-element.19), calls=%async_computation | async-start | bytes 262144 | tf_op jit(solution)/shard_map/all_to_all | solution.py:296
  17.6 58.8 %collective-permute-start = (f32[1032,256]{1,0:T(8,128)}, f32[1032,256]{1,0:T(8,128)S(1)}, u32[]{:S(2)}, u32[]{:S(2)}) collective-permute-start(f32[1032,256]{1,0:T(8,128)} %get-tuple-element.21), channel_id=1, source_target_pairs={{0,1},{1,0},{2,3},{3,2},{4,5},{5,4},{6,7},{7,6},{8,9},{9,8},{10,11... | collective-permute-start | bytes 3170312 | tf_op jit(solution)/shard_map/ppermute | solution.py:335
  46.7 14.9 %copy-start.2 = (f32[1,1024]{1,0:T(1,128)S(1)}, f32[1,1024]{1,0:T(1,128)}, u32[]{:S(2)}) copy-start(f32[1,1024]{1,0:T(1,128)} %get-tuple-element.25.sqx_ref) | copy-start | bytes 12292
  78.4 19.4 %copy-start.3 = (f32[1,1024]{1,0:T(1,128)S(1)}, f32[1,1024]{1,0:T(1,128)}, u32[]{:S(2)}) copy-start(f32[1,1024]{1,0:T(1,128)} %get-tuple-element.31.sqy_ref) | copy-start | bytes 12292

commit v4 on v3

--- a/solution.py
+++ b/solution.py
@@ -12,7 +12,7 @@
 SCALE = 128.0
 KAPPA = math.log2(math.e) / EPS / SCALE
 LOG2 = math.log2(math.e) / EPS
-LANES = 256
+LANES = 512
 SHARE = 32
 CHUNK = 2 * SHARE + 8
 
@@ -237,7 +237,7 @@
     y_other = wide_ref[0:n, :].astype(jnp.bfloat16)
     rows = as_rows(target_rows(in_lanes(wide_ref[n : n + n // width, :]), other, lc_ref[...]))
     chunks = out_ref.shape[0]
-    per = min(8, chunks)
+    per = min(16, chunks)
     for b in range(chunks // per):
         weights, downs = [], []
         for k in range(per):

time: 100 us -> 101 us (1.010)
  no operation moved by 1% of the time
where the time goes in v4:
time: 101 us; the launch traced here: 98.9 us
  blocking collectives  65.3 us (65%)
  starting transfers between devices  15.1 us (15%)
  Pallas kernels  10.7 us (11%)
  waiting for transfers between devices  7.11 us (7%)
    all_to_all x4, blocking collectives, exchange(): return lax.all_to_all(x, axis, 0, 0, axis_index_groups=groups, tiled=True)  65.3 us
    all_to_all x1, starting transfers between devices, exchange(): return lax.all_to_all(x, axis, 0, 0, axis_index_groups=groups, tiled=True)  12.9 us
    pallas_call x6, Pallas kernels, call(): pl.pallas_call(body, out_shape=outs, in_specs=specs, out_specs=out_specs,...  10.7 us
    all_to_all x1, waiting for transfers between devices, exchange(): return lax.all_to_all(x, axis, 0, 0, axis_index_groups=groups, tiled=True)  7.11 us
    ppermute x1, starting transfers between devices, on_device(): wide = lax.ppermute(wide, 'target', [(k, k ^ 1) for k in range(targets)])  2.14 us
  transfers between devices with their start and end apart: 2, of which 1 were waited for; matrix products, arithmetic and copies ran while one was open for 0% of the time, Pallas kernels for 4%

profile of v4, /device:TPU:1, one launch (start us, length us, event | category | flops | bytes accessed | tf_op | source)
XLA Modules:
  0.0 98.9 jit_solution(434979126604296250)
XLA Ops:
  0.6 0.0 copy-start
  0.6 0.0 copy-start.1
  0.7 0.0 copy-start.4
  0.7 0.0 copy-start.5
  0.7 0.0 copy-start.6
  0.7 4.0 %shard_map.76 = (f32[1032,256]{1,0:T(8,128)}, f32[32,8,128]{2,1,0:T(8,128)}, f32[1,1024]{1,0:T(1,128)}, f32[1,1024]{1,0:T(1,128)}) custom-call(bf16[1024,256]{1,0:T(8,128)(2,1)} %x_ref.3, bf16[1024,256]{1,0:T(8,128)(2,1)} %y_ref.3, s32[1,1024]{1,0:T(1,128)} %bitcast.5, s32[1,1024]{1,0:T(1,128)} %bitcast.8, f32[8,8]{1,0:T(8,128)} %lc_ref.3, s32[1]{0:T(128)} %bitcast.2.core_ref), custom_call_target="tpu_custom_call" | custom-call | flops 1073741824 | bytes 1048576 | tf_op jit(solution)/shard_map/pallas_call | solution.py:284
  4.7 12.9 %all-to-all-start = ((f32[32,8,128]{2,1,0:T(8,128)}), f32[32,8,128]{2,1,0:T(8,128)S(1)}, u32[]{:S(2)}, u32[]{:S(2)}) async-start(f32[32,8,128]{2,1,0:T(8,128)} %get-tuple-element.19), calls=%async_computation | async-start | bytes 262144 | tf_op jit(solution)/shard_map/all_to_all | solution.py:296
  17.6 2.1 %collective-permute-start = (f32[1032,256]{1,0:T(8,128)}, f32[1032,256]{1,0:T(8,128)S(1)}, u32[]{:S(2)}, u32[]{:S(2)}) collective-permute-start(f32[1032,256]{1,0:T(8,128)} %get-tuple-element.21), channel_id=1, source_target_pairs={{0,1},{1,0},{2,3},{3,2},{4,5},{5,4},{6,7},{7,6},{8,9},{9,8},{10,11... | collective-permute-start | bytes 3170312 | tf_op jit(solution)/shard_map/ppermute | solution.py:335
  19.8 7.1 %all-to-all-done.got_ref = f32[32,8,128]{2,1,0:T(8,128)S(1)} async-done(((f32[32,8,128]{2,1,0:T(8,128)}), f32[32,8,128]{2,1,0:T(8,128)S(1)}, u32[]{:S(2)}, u32[]{:S(2)}) %all-to-all-start) | async-done | bytes 131104 | tf_op jit(solution)/shard_map/all_to_all | solution.py:296
  26.9 0.0 copy-done
  26.9 0.0 copy-done.1
  26.9 0.0 copy-done.4
  26.9 0.0 copy-done.5
  26.9 0.0 copy-done.6
  26.9 2.1 %shard_map.77 = (f32[1024,1024]{1,0:T(8,128)S(1)}, f32[16,8,128]{2,1,0:T(8,128)S(1)}, f32[1,1024]{1,0:T(1,128)S(1)}) custom-call(bf16[1024,256]{1,0:T(8,128)(2,1)S(1)} %copy-done, bf16[1024,256]{1,0:T(8,128)(2,1)S(1)} %copy-done.1, s32[1,1024]{1,0:T(1,128)S(1)} %bitcast.6, s32[1,1024]{1,0:T(1,128)S(1)} %bitcast.9, f32[8,8]{1,0:T(8,128)S(1)} %copy-done.5, ...), custom_call_target="tpu_custom_call" | custom-call | flops 1073741824 | bytes 1048576 | tf_op jit(solution)/shard_map/pallas_call | solution.py:284
  29.0 17.8 %all_to_all.25.got_ref = f32[16,8,128]{2,1,0:T(8,128)S(1)} all-to-all(f32[16,8,128]{2,1,0:T(8,128)S(1)} %get-tuple-element.23), channel_id=1, replica_groups=mesh['train'=16,'target'=32] {'train'}, dimensions={0} | all-to-all | bytes 131072 | tf_op jit(solution)/shard_map/all_to_all | solution.py:296
  46.8 0.0 copy-start.2
  46.8 0.8 shard_map.78
  47.6 14.1 %all_to_all.26.got_ref = f32[32,8,128]{2,1,0:T(8,128)S(1)} all-to-all(f32[32,8,128]{2,1,0:T(8,128)S(1)} %get-tuple-element.26), channel_id=1, replica_groups=mesh['train'=16,'target'=32] {'target'}, dimensions={0} | all-to-all | bytes 262144 | tf_op jit(solution)/shard_map/all_to_all | solution.py:296
  61.7 0.0 copy-done.2
  61.7 0.8 shard_map.79
  62.4 14.0 %all_to_all.27.got_ref.columns_ref = f32[32,1,1152]{2,1,0:T(1,128)S(1)} all-to-all(f32[32,1,1152]{2,1,0:T(1,128)S(1)} %get-tuple-element.28), channel_id=1, replica_groups={{0,1,32,33,64,65,96,97,128,129,160,161,192,193,224,225,256,257,288,289,..., dimensions={0} | all-to-all | bytes 294912 | tf_op jit(solution)/shard_map/all_to_all | solution.py:296
  76.4 0.0 collective-permute-done.wide_ref
  76.4 2.3 %shard_map.80 = (f32[16,72,128]{2,1,0:T(8,128)S(1)}, f32[1,1024]{1,0:T(1,128)S(1)}) custom-call(f32[1024,1024]{1,0:T(8,128)S(1)} %get-tuple-element.20.t_ref, bf16[1024,256]{1,0:T(8,128)(2,1)S(1)} %copy-done, bf16[1024,256]{1,0:T(8,128)(2,1)S(1)} %copy-done.1, s32[1,1024]{1,0:T(1,128)S(1)} %bitcast.7, f32[8,8]{1,0:T(8,128)S(1)} %copy-done.5, ...), custom_call_target="tpu_custom_call" | custom-call | flops 1073741824 | bytes 1048576 | tf_op jit(solution)/shard_map/pallas_call | solution.py:284
  78.8 0.0 copy-start.3
  78.8 19.4 %all_to_all.28.got_ref = f32[16,72,128]{2,1,0:T(8,128)S(1)} all-to-all(f32[16,72,128]{2,1,0:T(8,128)S(1)} %get-tuple-element.29), channel_id=1, replica_groups={{0,2,4,6,8,10,12,14,16,18,20,22,24,26,28,30},{1,3,5,7,9,11,13,15,17,19,..., dimensions={0} | all-to-all | bytes 1179648 | tf_op jit(solution)/shard_map/all_to_all | solution.py:296
  98.2 0.0 copy-done.3
  98.2 0.7 shard_map.81
Async XLA Ops:
  0.6 26.3 %copy-start = (bf16[1024,256]{1,0:T(8,128)(2,1)S(1)}, bf16[1024,256]{1,0:T(8,128)(2,1)}, u32[]{:S(2)}) copy-start(bf16[1024,256]{1,0:T(8,128)(2,1)} %x_ref.3) | copy-start | bytes 1572868
  0.6 26.3 %copy-start.1 = (bf16[1024,256]{1,0:T(8,128)(2,1)S(1)}, bf16[1024,256]{1,0:T(8,128)(2,1)}, u32[]{:S(2)}) copy-start(bf16[1024,256]{1,0:T(8,128)(2,1)} %y_ref.3) | copy-start | bytes 1572868
  0.7 26.3 %copy-start.4 = (s32[1024]{0:T(1024)S(1)}, s32[1024]{0:T(1024)}, u32[]{:S(2)}) copy-start(s32[1024]{0:T(1024)} %param.6) | copy-start | bytes 12292
  0.7 26.3 %copy-start.5 = (f32[8,8]{1,0:T(8,128)S(1)}, f32[8,8]{1,0:T(8,128)}, u32[]{:S(2)}) copy-start(f32[8,8]{1,0:T(8,128)} %lc_ref.3) | copy-start | bytes 772
  0.7 26.3 %copy-start.6 = (s32[1024]{0:T(1024)S(1)}, s32[1024]{0:T(1024)}, u32[]{:S(2)}) copy-start(s32[1024]{0:T(1024)} %param.8) | copy-start | bytes 12292
  4.7 22.2 %all-to-all-start = ((f32[32,8,128]{2,1,0:T(8,128)}), f32[32,8,128]{2,1,0:T(8,128)S(1)}, u32[]{:S(2)}, u32[]{:S(2)}) async-start(f32[32,8,128]{2,1,0:T(8,128)} %get-tuple-element.19), calls=%async_computation | async-start | bytes 262144 | tf_op jit(solution)/shard_map/all_to_all | solution.py:296
  17.6 58.8 %collective-permute-start = (f32[1032,256]{1,0:T(8,128)}, f32[1032,256]{1,0:T(8,128)S(1)}, u32[]{:S(2)}, u32[]{:S(2)}) collective-permute-start(f32[1032,256]{1,0:T(8,128)} %get-tuple-element.21), channel_id=1, source_target_pairs={{0,1},{1,0},{2,3},{3,2},{4,5},{5,4},{6,7},{7,6},{8,9},{9,8},{10,11... | collective-permute-start | bytes 3170312 | tf_op jit(solution)/shard_map/ppermute | solution.py:335
  46.8 14.9 %copy-start.2 = (f32[1,1024]{1,0:T(1,128)S(1)}, f32[1,1024]{1,0:T(1,128)}, u32[]{:S(2)}) copy-start(f32[1,1024]{1,0:T(1,128)} %get-tuple-element.25.sqx_ref) | copy-start | bytes 12292
  78.8 19.4 %copy-start.3 = (f32[1,1024]{1,0:T(1,128)S(1)}, f32[1,1024]{1,0:T(1,128)}, u32[]{:S(2)}) copy-start(f32[1,1024]{1,0:T(1,128)} %get-tuple-element.31.sqy_ref) | copy-start | bytes 12292

commit v5 on v3

--- a/solution.py
+++ b/solution.py
@@ -237,7 +237,7 @@
     y_other = wide_ref[0:n, :].astype(jnp.bfloat16)
     rows = as_rows(target_rows(in_lanes(wide_ref[n : n + n // width, :]), other, lc_ref[...]))
     chunks = out_ref.shape[0]
-    per = min(8, chunks)
+    per = min(4, chunks)
     for b in range(chunks // per):
         weights, downs = [], []
         for k in range(per):

time: 100 us -> 101 us (1.010)
  no operation moved by 1% of the time
where the time goes in v5:
time: 101 us; the launch traced here: 99 us
  blocking collectives  65.3 us (65%)
  starting transfers between devices  15.1 us (15%)
  Pallas kernels  10.8 us (11%)
  waiting for transfers between devices  7.11 us (7%)
    all_to_all x4, blocking collectives, exchange(): return lax.all_to_all(x, axis, 0, 0, axis_index_groups=groups, tiled=True)  65.3 us
    all_to_all x1, starting transfers between devices, exchange(): return lax.all_to_all(x, axis, 0, 0, axis_index_groups=groups, tiled=True)  12.9 us
    pallas_call x6, Pallas kernels, call(): pl.pallas_call(body, out_shape=outs, in_specs=specs, out_specs=out_specs,...  10.8 us
    all_to_all x1, waiting for transfers between devices, exchange(): return lax.all_to_all(x, axis, 0, 0, axis_index_groups=groups, tiled=True)  7.11 us
    ppermute x1, starting transfers between devices, on_device(): wide = lax.ppermute(wide, 'target', [(k, k ^ 1) for k in range(targets)])  2.14 us
  transfers between devices with their start and end apart: 2, of which 1 were waited for; matrix products, arithmetic and copies ran while one was open for 0% of the time, Pallas kernels for 4%

profile of v5, /device:TPU:1, one launch (start us, length us, event | category | flops | bytes accessed | tf_op | source)
XLA Modules:
  0.0 99.0 jit_solution(9775110830367411711)
XLA Ops:
  0.6 0.0 copy-start
  0.6 0.0 copy-start.1
  0.7 0.0 copy-start.4
  0.7 0.0 copy-start.5
  0.7 0.0 copy-start.6
  0.7 4.0 %shard_map.76 = (f32[1032,256]{1,0:T(8,128)}, f32[32,8,128]{2,1,0:T(8,128)}, f32[1,1024]{1,0:T(1,128)}, f32[1,1024]{1,0:T(1,128)}) custom-call(bf16[1024,256]{1,0:T(8,128)(2,1)} %x_ref.3, bf16[1024,256]{1,0:T(8,128)(2,1)} %y_ref.3, s32[1,1024]{1,0:T(1,128)} %bitcast.5, s32[1,1024]{1,0:T(1,128)} %bitcast.8, f32[8,8]{1,0:T(8,128)} %lc_ref.3, s32[1]{0:T(128)} %bitcast.2.core_ref), custom_call_target="tpu_custom_call" | custom-call | flops 1073741824 | bytes 1048576 | tf_op jit(solution)/shard_map/pallas_call | solution.py:284
  4.7 12.9 %all-to-all-start = ((f32[32,8,128]{2,1,0:T(8,128)}), f32[32,8,128]{2,1,0:T(8,128)S(1)}, u32[]{:S(2)}, u32[]{:S(2)}) async-start(f32[32,8,128]{2,1,0:T(8,128)} %get-tuple-element.19), calls=%async_computation | async-start | bytes 262144 | tf_op jit(solution)/shard_map/all_to_all | solution.py:296
  17.6 2.1 %collective-permute-start = (f32[1032,256]{1,0:T(8,128)}, f32[1032,256]{1,0:T(8,128)S(1)}, u32[]{:S(2)}, u32[]{:S(2)}) collective-permute-start(f32[1032,256]{1,0:T(8,128)} %get-tuple-element.21), channel_id=1, source_target_pairs={{0,1},{1,0},{2,3},{3,2},{4,5},{5,4},{6,7},{7,6},{8,9},{9,8},{10,11... | collective-permute-start | bytes 3170312 | tf_op jit(solution)/shard_map/ppermute | solution.py:335
  19.8 7.1 %all-to-all-done.got_ref = f32[32,8,128]{2,1,0:T(8,128)S(1)} async-done(((f32[32,8,128]{2,1,0:T(8,128)}), f32[32,8,128]{2,1,0:T(8,128)S(1)}, u32[]{:S(2)}, u32[]{:S(2)}) %all-to-all-start) | async-done | bytes 131104 | tf_op jit(solution)/shard_map/all_to_all | solution.py:296
  26.9 0.0 copy-done
  26.9 0.0 copy-done.1
  26.9 0.0 copy-done.4
  26.9 0.0 copy-done.5
  26.9 0.0 copy-done.6
  26.9 2.0 %shard_map.77 = (f32[1024,1024]{1,0:T(8,128)S(1)}, f32[16,8,128]{2,1,0:T(8,128)S(1)}, f32[1,1024]{1,0:T(1,128)S(1)}) custom-call(bf16[1024,256]{1,0:T(8,128)(2,1)S(1)} %copy-done, bf16[1024,256]{1,0:T(8,128)(2,1)S(1)} %copy-done.1, s32[1,1024]{1,0:T(1,128)S(1)} %bitcast.6, s32[1,1024]{1,0:T(1,128)S(1)} %bitcast.9, f32[8,8]{1,0:T(8,128)S(1)} %copy-done.5, ...), custom_call_target="tpu_custom_call" | custom-call | flops 1073741824 | bytes 1048576 | tf_op jit(solution)/shard_map/pallas_call | solution.py:284
  29.0 17.8 %all_to_all.25.got_ref = f32[16,8,128]{2,1,0:T(8,128)S(1)} all-to-all(f32[16,8,128]{2,1,0:T(8,128)S(1)} %get-tuple-element.23), channel_id=1, replica_groups=mesh['train'=16,'target'=32] {'train'}, dimensions={0} | all-to-all | bytes 131072 | tf_op jit(solution)/shard_map/all_to_all | solution.py:296
  46.7 0.0 copy-start.2
  46.7 0.8 shard_map.78
  47.5 14.1 %all_to_all.26.got_ref = f32[32,8,128]{2,1,0:T(8,128)S(1)} all-to-all(f32[32,8,128]{2,1,0:T(8,128)S(1)} %get-tuple-element.26), channel_id=1, replica_groups=mesh['train'=16,'target'=32] {'target'}, dimensions={0} | all-to-all | bytes 262144 | tf_op jit(solution)/shard_map/all_to_all | solution.py:296
  61.6 0.0 copy-done.2
  61.6 0.8 shard_map.79
  62.4 14.0 %all_to_all.27.got_ref.columns_ref = f32[32,1,1152]{2,1,0:T(1,128)S(1)} all-to-all(f32[32,1,1152]{2,1,0:T(1,128)S(1)} %get-tuple-element.28), channel_id=1, replica_groups={{0,1,32,33,64,65,96,97,128,129,160,161,192,193,224,225,256,257,288,289,..., dimensions={0} | all-to-all | bytes 294912 | tf_op jit(solution)/shard_map/all_to_all | solution.py:296
  76.4 0.0 collective-permute-done.wide_ref
  76.4 2.5 %shard_map.80 = (f32[16,72,128]{2,1,0:T(8,128)S(1)}, f32[1,1024]{1,0:T(1,128)S(1)}) custom-call(f32[1024,1024]{1,0:T(8,128)S(1)} %get-tuple-element.20.t_ref, bf16[1024,256]{1,0:T(8,128)(2,1)S(1)} %copy-done, bf16[1024,256]{1,0:T(8,128)(2,1)S(1)} %copy-done.1, s32[1,1024]{1,0:T(1,128)S(1)} %bitcast.7, f32[8,8]{1,0:T(8,128)S(1)} %copy-done.5, ...), custom_call_target="tpu_custom_call" | custom-call | flops 1073741824 | bytes 1048576 | tf_op jit(solution)/shard_map/pallas_call | solution.py:284
  78.9 0.0 copy-start.3
  78.9 19.4 %all_to_all.28.got_ref = f32[16,72,128]{2,1,0:T(8,128)S(1)} all-to-all(f32[16,72,128]{2,1,0:T(8,128)S(1)} %get-tuple-element.29), channel_id=1, replica_groups={{0,2,4,6,8,10,12,14,16,18,20,22,24,26,28,30},{1,3,5,7,9,11,13,15,17,19,..., dimensions={0} | all-to-all | bytes 1179648 | tf_op jit(solution)/shard_map/all_to_all | solution.py:296
  98.3 0.0 copy-done.3
  98.3 0.7 shard_map.81
Async XLA Ops:
  0.6 26.3 %copy-start = (bf16[1024,256]{1,0:T(8,128)(2,1)S(1)}, bf16[1024,256]{1,0:T(8,128)(2,1)}, u32[]{:S(2)}) copy-start(bf16[1024,256]{1,0:T(8,128)(2,1)} %x_ref.3) | copy-start | bytes 1572868
  0.6 26.3 %copy-start.1 = (bf16[1024,256]{1,0:T(8,128)(2,1)S(1)}, bf16[1024,256]{1,0:T(8,128)(2,1)}, u32[]{:S(2)}) copy-start(bf16[1024,256]{1,0:T(8,128)(2,1)} %y_ref.3) | copy-start | bytes 1572868
  0.7 26.3 %copy-start.4 = (s32[1024]{0:T(1024)S(1)}, s32[1024]{0:T(1024)}, u32[]{:S(2)}) copy-start(s32[1024]{0:T(1024)} %param.6) | copy-start | bytes 12292
  0.7 26.3 %copy-start.5 = (f32[8,8]{1,0:T(8,128)S(1)}, f32[8,8]{1,0:T(8,128)}, u32[]{:S(2)}) copy-start(f32[8,8]{1,0:T(8,128)} %lc_ref.3) | copy-start | bytes 772
  0.7 26.3 %copy-start.6 = (s32[1024]{0:T(1024)S(1)}, s32[1024]{0:T(1024)}, u32[]{:S(2)}) copy-start(s32[1024]{0:T(1024)} %param.8) | copy-start | bytes 12292
  4.7 22.2 %all-to-all-start = ((f32[32,8,128]{2,1,0:T(8,128)}), f32[32,8,128]{2,1,0:T(8,128)S(1)}, u32[]{:S(2)}, u32[]{:S(2)}) async-start(f32[32,8,128]{2,1,0:T(8,128)} %get-tuple-element.19), calls=%async_computation | async-start | bytes 262144 | tf_op jit(solution)/shard_map/all_to_all | solution.py:296
  17.6 58.8 %collective-permute-start = (f32[1032,256]{1,0:T(8,128)}, f32[1032,256]{1,0:T(8,128)S(1)}, u32[]{:S(2)}, u32[]{:S(2)}) collective-permute-start(f32[1032,256]{1,0:T(8,128)} %get-tuple-element.21), channel_id=1, source_target_pairs={{0,1},{1,0},{2,3},{3,2},{4,5},{5,4},{6,7},{7,6},{8,9},{9,8},{10,11... | collective-permute-start | bytes 3170312 | tf_op jit(solution)/shard_map/ppermute | solution.py:335
  46.7 14.9 %copy-start.2 = (f32[1,1024]{1,0:T(1,128)S(1)}, f32[1,1024]{1,0:T(1,128)}, u32[]{:S(2)}) copy-start(f32[1,1024]{1,0:T(1,128)} %get-tuple-element.25.sqx_ref) | copy-start | bytes 12292
  78.9 19.4 %copy-start.3 = (f32[1,1024]{1,0:T(1,128)S(1)}, f32[1,1024]{1,0:T(1,128)}, u32[]{:S(2)}) copy-start(f32[1,1024]{1,0:T(1,128)} %get-tuple-element.31.sqy_ref) | copy-start | bytes 12292
